TPU v7x, 512 devices: a whole 4x4x16 slice. The times are simulated.
512 devices in a mesh: grp: 16 (over x, y), dev: 32 (over z, core).
Axes of the slice: x: 4, y: 4, z: 16, core: 2. Of those that a mesh axis runs over, the one named last changes fastest.
Arguments:
- right_side: float32 [3584, 22, 896], P(('grp', 'dev')), may hold values from -9 to 9
- screening: float32 [3584, 22, 896], P(('grp', 'dev')), may hold values from 0.01 to 8
Outputs:
- solution_field: float32 [3584, 22, 896], P(('grp', 'dev'))
- residual: float32 [3584, 22, 896], P(('grp', 'dev'))
All inputs are finite; a program needn't handle non-finite values.
Results may differ from a plain program's by a relative error of at most 0.0003.
Values sent between devices are 32-bit elements; how exact they have to be, the bound alone decides.
No kernel may reach another device: no remote copies, remote signals or barrier semaphores. Data moves between devices by JAX's collectives and lax.ppermute only.
A program may use at most 64 MiB of HBM per device.

v0:
```python
import jax
import jax.numpy as jnp
import numpy as np
from jax import lax
from jax.sharding import PartitionSpec as P

ITERS = 2
CSWEEPS = 3


damping = 0.6


def from_behind(block, axis, distance):
    devices = range(lax.axis_size(axis))
    route = [((i - distance) % len(devices), i) for i in devices]
    return lax.ppermute(block, axis, route)


def with_halo(block, sides, width):
    for axis, dim in sides:
        count = lax.axis_size(axis)
        forward = [(i, i + 1) for i in range(count - 1)]
        forward.append((count - 1, 0))
        backward = [(target, source) for source, target in forward]
        low = lax.ppermute(
            lax.slice_in_dim(block, block.shape[dim] - width, None, axis=dim), axis, forward
        )
        high = lax.ppermute(lax.slice_in_dim(block, 0, width, axis=dim), axis, backward)
        block = jnp.concatenate([low, block, high], axis=dim)
    return block


def legendre_seven(points):
    return (429.0 * points**7 - 693.0 * points**5 + 315.0 * points**3 - 35.0 * points) / 16.0


def pad_vector(vector, before, after):
    return np.concatenate([np.zeros(before), vector, np.zeros(after)])


def pad_matrix(matrix, before, after):
    width = matrix.shape[1]
    rows = np.concatenate([np.zeros((before, width)), matrix, np.zeros((after, width))], axis=0)
    height = rows.shape[0]
    return np.concatenate([np.zeros((height, before)), rows, np.zeros((height, after))], axis=1)


def diag_entries(matrix):
    return np.array([matrix[k, k] for k in range(matrix.shape[0])])


def diag_matrix(vector):
    count = vector.shape[0]
    return np.stack([pad_vector(np.array([vector[k]]), k, count - 1 - k) for k in range(count)])


def gll_tables():
    gll_nodes = np.array(
        [
            -1.0,
            -0.8717401485096066,
            -0.5917001814331423,
            -0.2092992179024789,
            0.2092992179024789,
            0.5917001814331423,
            0.8717401485096066,
            1.0,
        ]
    )
    values = legendre_seven(gll_nodes)
    weights = 2.0 / (56.0 * values * values)
    spacing = gll_nodes[:, None] - gll_nodes[None, :]
    distinct = np.abs(spacing) > 1e-12
    divisor = np.where(distinct, spacing, 1.0)
    derivative = np.where(distinct, values[:, None] / values[None, :] / divisor, 0.0)
    derivative = derivative + diag_matrix(np.array([-14.0, 0.0, 0.0, 0.0, 0.0, 0.0, 0.0, 14.0]))
    stiffness = derivative.T @ (weights[:, None] * derivative)
    return (gll_nodes, weights, stiffness)


def tables(elems_y):
    gll_nodes, weights, stiffness = gll_tables()
    count_y = 7 * elems_y + 1
    mass_y = np.zeros(count_y)
    stiff_y = np.zeros((count_y, count_y))
    coarse_stiff_y = np.zeros((elems_y + 1, elems_y + 1))
    pair_stiff = np.array([[0.5, -0.5], [-0.5, 0.5]])
    phi_low = (1.0 - gll_nodes) / 2.0
    phi_high = (1.0 + gll_nodes) / 2.0
    for element in range(elems_y):
        before = 7 * element
        trailing = count_y - 8 - before
        mass_y = mass_y + pad_vector(weights, before, trailing)
        stiff_y = stiff_y + pad_matrix(stiffness, before, trailing)
        coarse_stiff_y = coarse_stiff_y + pad_matrix(pair_stiff, element, elems_y - 1 - element)
    row_list = []
    for node_index in range(count_y):
        element = min(node_index // 7, elems_y - 1)
        offset = node_index - 7 * element
        row_list.append(
            pad_vector(
                np.array([phi_low[offset], phi_high[offset]]), element, elems_y - 1 - element
            )
        )
    interp_y = np.stack(row_list)
    stiff_diag = diag_entries(stiffness)
    mass_edge = np.concatenate([np.array([weights[0] + weights[7]]), weights[1:7]])
    stiff_edge = np.concatenate([np.array([stiff_diag[0] + stiff_diag[7]]), stiff_diag[1:7]])
    coarse_mass_y = np.concatenate([np.array([1.0]), np.full(elems_y - 1, 2.0), np.array([1.0])])
    entry_list = [
        stiffness,
        mass_edge,
        stiff_edge,
        mass_y,
        stiff_y,
        diag_entries(stiff_y),
        interp_y,
        phi_low[:7],
        phi_high[:7],
        coarse_stiff_y,
        coarse_mass_y,
        diag_entries(coarse_stiff_y),
    ]
    return [jnp.asarray(entry_table, jnp.float32) for entry_table in entry_list]


def stiff_along_y(grid_values, stiff_y):
    return jnp.einsum("mn,xnz->xmz", stiff_y, grid_values, precision=lax.Precision.HIGHEST)


def stiff_along_z(grid_values, stiffness):
    planes, count_y, count_z = grid_values.shape
    blocks = grid_values.reshape(planes, count_y, 7, count_z // 7)
    extended = jnp.concatenate([blocks, jnp.roll(blocks[:, :, :1], -1, axis=3)], axis=2)
    product = jnp.einsum("ij,xyjz->xyiz", stiffness, extended, precision=lax.Precision.HIGHEST)
    folded = jnp.concatenate(
        [product[:, :, :1] + jnp.roll(product[:, :, 7:8], 1, axis=3), product[:, :, 1:7]], axis=2
    )
    return folded.reshape(planes, count_y, count_z)


def combine(grid_values, screening, stiff_x_part, mass_x, tables_list):
    stiffness, mass_edge, stiff_y = (tables_list[0], tables_list[1], tables_list[4])
    mass_z = jnp.repeat(mass_edge, grid_values.shape[2] // 7)[None, None, :]
    mass_yy = tables_list[3][None, :, None]
    mass_xx = mass_x[:, None, None]
    return (
        mass_xx * mass_yy * mass_z * screening * grid_values
        + mass_yy * mass_z * stiff_x_part
        + mass_xx * mass_z * stiff_along_y(grid_values, stiff_y)
        + mass_xx * mass_yy * stiff_along_z(grid_values, stiffness)
    )


def diagonal(screening, mass_x, stiff_x_diag, tables_list):
    elems_z = screening.shape[2] // 7
    mass_z = jnp.repeat(tables_list[1], elems_z)[None, None, :]
    stiff_z_diag = jnp.repeat(tables_list[2], elems_z)[None, None, :]
    mass_yy = tables_list[3][None, :, None]
    stiff_y_diag = tables_list[5][None, :, None]
    mass_xx = mass_x[:, None, None]
    return (
        mass_xx * mass_yy * mass_z * screening
        + mass_yy * mass_z * stiff_x_diag[:, None, None]
        + mass_xx * mass_z * stiff_y_diag
        + mass_xx * mass_yy * stiff_z_diag
    )


def restrict_yz(grid_values, tables_list):
    planes, count_y, count_z = grid_values.shape
    element_view = grid_values.reshape(planes, count_y, 7, count_z // 7)
    share_low = jnp.einsum(
        "i,xyiz->xyz", tables_list[7], element_view, precision=lax.Precision.HIGHEST
    )
    share_high = jnp.einsum(
        "i,xyiz->xyz", tables_list[8], element_view, precision=lax.Precision.HIGHEST
    )
    along_z = share_low + jnp.roll(share_high, 1, axis=2)
    return jnp.einsum("mv,xmz->xvz", tables_list[6], along_z, precision=lax.Precision.HIGHEST)


def prolong_yz(coarse_x, tables_list):
    fine_y = jnp.einsum("mv,xvz->xmz", tables_list[6], coarse_x, precision=lax.Precision.HIGHEST)
    phi_low = tables_list[7][None, None, :, None]
    phi_high = tables_list[8][None, None, :, None]
    fine_z = (
        phi_low * fine_y[:, :, None, :] + phi_high * jnp.roll(fine_y, -1, axis=2)[:, :, None, :]
    )
    planes, count_y, elems_z = fine_y.shape
    return fine_z.reshape(planes, count_y, 7 * elems_z)


def coarse_operator(values, lower_values, upper_values, coarse_screen, tables_list):
    mass_cy = tables_list[10][:, None]
    along_y = jnp.einsum("uv,...vz->...uz", tables_list[9], values, precision=lax.Precision.HIGHEST)
    along_z = values - 0.5 * (jnp.roll(values, 1, axis=-1) + jnp.roll(values, -1, axis=-1))
    along_x = values - 0.5 * (lower_values + upper_values)
    return (
        4.0 * mass_cy * coarse_screen * values
        + 2.0 * mass_cy * along_x
        + 4.0 * along_y
        + 2.0 * mass_cy * along_z
    )


def coarse_diagonal(coarse_screen, tables_list):
    mass_cy = tables_list[10][:, None]
    return 4.0 * mass_cy * coarse_screen + 4.0 * mass_cy + 4.0 * tables_list[11][:, None]


def jacobi(coarse_rhs, coarse_screen, neighbours, tables_list):
    diag_c = coarse_diagonal(coarse_screen, tables_list)
    solution = damping * coarse_rhs / diag_c
    for sweep_index in range(CSWEEPS - 1):
        lower_values, upper_values = neighbours(solution)
        solution = (
            solution
            + damping
            * (
                coarse_rhs
                - coarse_operator(solution, lower_values, upper_values, coarse_screen, tables_list)
            )
            / diag_c
        )
    return solution


def apply_operator(grid_values, screening, tables_list):
    top_plane = from_behind(grid_values[0:1], ("grp", "dev"), -1)
    extended = jnp.concatenate([grid_values, top_plane], axis=0)
    product = jnp.einsum("ij,jyz->iyz", tables_list[0], extended, precision=lax.Precision.HIGHEST)
    returned = from_behind(product[7:8], ("grp", "dev"), 1)
    stiff_x_part = jnp.concatenate([product[0:1] + returned, product[1:7]], axis=0)
    return combine(grid_values, screening, stiff_x_part, tables_list[1], tables_list)


def coarse_solve(coarse_rhs, coarse_screen, tables_list):

    def neighbours(values):
        padded = with_halo(values[None], ((("grp", "dev"), 0),), 1)
        return (padded[0], padded[2])

    solution = jacobi(coarse_rhs, coarse_screen, neighbours, tables_list)
    unused_lower, upper_values = neighbours(solution)
    return (solution, upper_values)


def precondition(residual, screening, diag_a, tables_list):
    along_y = restrict_yz(residual, tables_list)
    share_low = jnp.einsum("i,ivz->vz", tables_list[7], along_y, precision=lax.Precision.HIGHEST)
    share_high = jnp.einsum("i,ivz->vz", tables_list[8], along_y, precision=lax.Precision.HIGHEST)
    incoming = from_behind(share_high, ("grp", "dev"), 1)
    coarse_rhs = share_low + incoming
    elems_z = residual.shape[2] // 7
    coarse_screen = screening[0, ::7, :elems_z]
    mine_values, upper_values = coarse_solve(coarse_rhs, coarse_screen, tables_list)
    fine_x = (
        tables_list[7][:, None, None] * mine_values[None]
        + tables_list[8][:, None, None] * upper_values[None]
    )
    return residual / diag_a + prolong_yz(fine_x, tables_list)


def residual_dot(first, second):
    return lax.psum(jnp.sum(first * second), ("grp", "dev"))


def per_device(right_side, screening):
    tables_list = tables((right_side.shape[1] - 1) // 7)
    diag_a = diagonal(screening, tables_list[1], tables_list[2], tables_list)
    solution_field = jnp.zeros_like(right_side)
    residual = right_side
    precond = precondition(residual, screening, diag_a, tables_list)
    direction = precond
    rho_now = residual_dot(residual, precond)
    for iteration in range(ITERS):
        operated = apply_operator(direction, screening, tables_list)
        step_length = rho_now / lax.psum(jnp.sum(direction * operated), ("grp", "dev"))
        solution_field = solution_field + step_length * direction
        residual = residual - step_length * operated
        if iteration + 1 < ITERS:
            precond = precondition(residual, screening, diag_a, tables_list)
            rho_next = residual_dot(residual, precond)
            direction = precond + rho_next / rho_now * direction
            rho_now = rho_next
    return (solution_field, residual)


def solution(mesh):
    in_specs = (P(("grp", "dev"), None, None), P(("grp", "dev"), None, None))
    out_specs = (P(("grp", "dev"), None, None), P(("grp", "dev"), None, None))
    return jax.shard_map(
        per_device, mesh=mesh, in_specs=in_specs, out_specs=out_specs, check_vma=False
    )
```

profile of v0, /device:TPU:1, one launch (start us, length us, event | category | flops | bytes accessed | tf_op | source)
XLA Modules:
  0.0 467.7 jit_solution(1766438189371855155)
XLA Ops:
  4.7 5.1 %collective-permute-start = (f32[4,128]{1,0:T(4,128)S(1)}, f32[4,128]{1,0:T(4,128)S(1)}, u32[]{:S(2)}, u32[]{:S(2)}) collective-permute-start(f32[4,128]{1,0:T(4,128)S(1)} %bitcast.218), channel_id=1, source_target_pairs={{511,0},{0,1},{1,2},{2,3},{3,4},{4,5},{5,6},{6,7},{7,8},{8,9},{9,1... | collective-permute-start | bytes 6152 | tf_op jit(solution)/shard_map/ppermute | solution.py:17
  10.8 3.4 collective-permute-done
  14.3 1.9 collective-permute-start.1
  16.2 10.7 %collective-permute-start.2 = (f32[1,4,128]{2,1,0:T(4,128)S(1)}, f32[1,4,128]{2,1,0:T(4,128)S(1)}, u32[]{:S(2)}, u32[]{:S(2)}) collective-permute-start(f32[1,4,128]{2,1,0:T(4,128)S(1)} %bitcast.209), channel_id=1, source_target_pairs={{1,0},{2,1},{3,2},{4,3},{5,4},{6,5},{7,6},{8,7},{9,8},{10,9},{11,1... | collective-permute-start | bytes 6152 | tf_op jit(solution)/shard_map/ppermute | solution.py:29
  28.6 1.9 collective-permute-start.3
  30.5 9.6 %collective-permute-start.4 = (f32[1,4,128]{2,1,0:T(4,128)S(1)}, f32[1,4,128]{2,1,0:T(4,128)S(1)}, u32[]{:S(2)}, u32[]{:S(2)}) collective-permute-start(f32[1,4,128]{2,1,0:T(4,128)S(1)} %bitcast.215), channel_id=1, source_target_pairs={{1,0},{2,1},{3,2},{4,3},{5,4},{6,5},{7,6},{8,7},{9,8},{10,9},{11,1... | collective-permute-start | bytes 6152 | tf_op jit(solution)/shard_map/ppermute | solution.py:29
  41.0 9.7 %collective-permute-start.5 = (f32[1,4,128]{2,1,0:T(4,128)S(1)}, f32[1,4,128]{2,1,0:T(4,128)S(1)}, u32[]{:S(2)}, u32[]{:S(2)}) collective-permute-start(f32[1,4,128]{2,1,0:T(4,128)S(1)} %bitcast.221), channel_id=1, source_target_pairs={{1,0},{2,1},{3,2},{4,3},{5,4},{6,5},{7,6},{8,7},{9,8},{10,9},{11,1... | collective-permute-start | bytes 6152 | tf_op jit(solution)/shard_map/ppermute | solution.py:29
  56.5 9.5 %collective-permute-start.6 = (f32[1,22,896]{2,0,1:T(1,128)S(1)}, f32[1,22,896]{2,0,1:T(1,128)S(1)}, u32[]{:S(2)}, u32[]{:S(2)}) collective-permute-start(f32[1,22,896]{2,0,1:T(1,128)S(1)} %slice.209), channel_id=1, source_target_pairs={{1,0},{2,1},{3,2},{4,3},{5,4},{6,5},{7,6},{8,7},{9,8},{10,9},{11,1... | collective-permute-start | bytes 236552 | tf_op jit(solution)/shard_map/ppermute | solution.py:17
  69.3 1.9 collective-permute-start.7
  72.3 6.7 %collective-permute-done.7 = f32[1,22,896]{2,0,1:T(1,128)S(1)} collective-permute-done((f32[1,22,896]{2,0,1:T(1,128)S(1)}, f32[1,22,896]{2,0,1:T(1,128)S(1)}, u32[]{:S(2)}, u32[]{:S(2)}) %collective-permute-start.7) | collective-permute-done | bytes 78880 | tf_op jit(solution)/shard_map/ppermute | solution.py:17
  80.6 105.0 %all-reduce = (f32[]{:T(128)}, f32[]{:T(128)}) all-reduce(f32[]{:T(128)} %get-tuple-element.7, f32[]{:T(128)} %get-tuple-element.6), channel_id=1, replica_groups=mesh['grp'=16,'dev'=32] {'grp','dev'}, use_global_device_ids=true, to_apply=%region_1.2 | all-reduce | flops 2 | bytes 16 | tf_op jit(solution)/shard_map/psum | solution.py:267
  189.0 4.2 collective-permute-start.8
  194.0 7.9 %collective-permute-start.10 = (f32[1,4,128]{2,1,0:T(4,128)S(1)}, f32[1,4,128]{2,1,0:T(4,128)S(1)}, u32[]{:S(2)}, u32[]{:S(2)}) collective-permute-start(f32[1,4,128]{2,1,0:T(4,128)S(1)} %bitcast.210), channel_id=1, source_target_pairs={{1,0},{2,1},{3,2},{4,3},{5,4},{6,5},{7,6},{8,7},{9,8},{10,9},{11,1... | collective-permute-start | bytes 6152 | tf_op jit(solution)/shard_map/ppermute | solution.py:29
  202.0 1.9 collective-permute-start.9
  205.1 3.8 collective-permute-start.11
  208.9 7.3 %collective-permute-start.12 = (f32[1,4,128]{2,1,0:T(4,128)S(1)}, f32[1,4,128]{2,1,0:T(4,128)S(1)}, u32[]{:S(2)}, u32[]{:S(2)}) collective-permute-start(f32[1,4,128]{2,1,0:T(4,128)S(1)} %bitcast.213), channel_id=1, source_target_pairs={{1,0},{2,1},{3,2},{4,3},{5,4},{6,5},{7,6},{8,7},{9,8},{10,9},{11,1... | collective-permute-start | bytes 6152 | tf_op jit(solution)/shard_map/ppermute | solution.py:29
  217.2 9.7 %collective-permute-start.13 = (f32[1,4,128]{2,1,0:T(4,128)S(1)}, f32[1,4,128]{2,1,0:T(4,128)S(1)}, u32[]{:S(2)}, u32[]{:S(2)}) collective-permute-start(f32[1,4,128]{2,1,0:T(4,128)S(1)} %bitcast.220), channel_id=1, source_target_pairs={{1,0},{2,1},{3,2},{4,3},{5,4},{6,5},{7,6},{8,7},{9,8},{10,9},{11,1... | collective-permute-start | bytes 6152 | tf_op jit(solution)/shard_map/ppermute | solution.py:29
  230.0 2.6 multiply_reduce_fusion.1
  232.7 110.7 %psum.30 = f32[]{:T(128)} all-reduce(f32[]{:T(128)} %get-tuple-element.12), channel_id=1, replica_groups=mesh['grp'=16,'dev'=32] {'grp','dev'}, use_global_device_ids=true, to_apply=%region_5.6 | all-reduce | flops 1 | bytes 8 | tf_op jit(solution)/shard_map/psum | solution.py:267
  348.0 3.1 collective-permute-start.14
  351.4 2.3 collective-permute-done.14
  354.5 1.9 collective-permute-start.15
  357.4 2.0 reshape.162
  361.9 102.5 %psum.31 = f32[]{:T(128)} all-reduce(f32[]{:T(128)} %get-tuple-element.10), channel_id=1, replica_groups=mesh['grp'=16,'dev'=32] {'grp','dev'}, use_global_device_ids=true, to_apply=%region_7.8 | all-reduce | flops 1 | bytes 8 | tf_op jit(solution)/shard_map/psum | solution.py:280
  (153 shorter events, 37.0 us)
Async XLA Ops:
  3.2 7.6 %copy-start = (f32[7,22,896]{2,1,0:T(8,128)S(1)}, f32[7,22,896]{2,1,0:T(8,128)}, u32[]{:S(2)}) copy-start(f32[7,22,896]{2,1,0:T(8,128)} %param.15) | copy-start | bytes 1655812
  4.6 5.2 %copy-start.10 = (f32[7]{0:T(128)S(1)}, f32[7]{0:T(128)}, u32[]{:S(2)}) copy-start(f32[7]{0:T(128)} %constant.37.clone) | copy-start | bytes 88
  4.6 5.2 %copy-start.11 = (f32[7]{0:T(128)S(1)}, f32[7]{0:T(128)}, u32[]{:S(2)}) copy-start(f32[7]{0:T(128)} %constant.36.clone) | copy-start | bytes 88
  4.7 9.6 %collective-permute-start = (f32[4,128]{1,0:T(4,128)S(1)}, f32[4,128]{1,0:T(4,128)S(1)}, u32[]{:S(2)}, u32[]{:S(2)}) collective-permute-start(f32[4,128]{1,0:T(4,128)S(1)} %bitcast.218), channel_id=1, source_target_pairs={{511,0},{0,1},{1,2},{2,3},{3,4},{4,5},{5,6},{6,7},{7,8},{8,9},{9,1... | collective-permute-start | bytes 6152 | tf_op jit(solution)/shard_map/ppermute | solution.py:17
  14.3 12.8 %collective-permute-start.1 = (f32[1,4,128]{2,1,0:T(4,128)S(1)}, f32[1,4,128]{2,1,0:T(4,128)S(1)}, u32[]{:S(2)}, u32[]{:S(2)}) collective-permute-start(f32[1,4,128]{2,1,0:T(4,128)S(1)} %bitcast.208), channel_id=1, source_target_pairs={{0,1},{1,2},{2,3},{3,4},{4,5},{5,6},{6,7},{7,8},{8,9},{9,10},{10,1... | collective-permute-start | bytes 6152 | tf_op jit(solution)/shard_map/ppermute | solution.py:26
  16.2 11.5 %collective-permute-start.2 = (f32[1,4,128]{2,1,0:T(4,128)S(1)}, f32[1,4,128]{2,1,0:T(4,128)S(1)}, u32[]{:S(2)}, u32[]{:S(2)}) collective-permute-start(f32[1,4,128]{2,1,0:T(4,128)S(1)} %bitcast.209), channel_id=1, source_target_pairs={{1,0},{2,1},{3,2},{4,3},{5,4},{6,5},{7,6},{8,7},{9,8},{10,9},{11,1... | collective-permute-start | bytes 6152 | tf_op jit(solution)/shard_map/ppermute | solution.py:29
  28.6 11.6 %collective-permute-start.3 = (f32[1,4,128]{2,1,0:T(4,128)S(1)}, f32[1,4,128]{2,1,0:T(4,128)S(1)}, u32[]{:S(2)}, u32[]{:S(2)}) collective-permute-start(f32[1,4,128]{2,1,0:T(4,128)S(1)} %bitcast.214), channel_id=1, source_target_pairs={{0,1},{1,2},{2,3},{3,4},{4,5},{5,6},{6,7},{7,8},{8,9},{9,10},{10,1... | collective-permute-start | bytes 6152 | tf_op jit(solution)/shard_map/ppermute | solution.py:26
  30.5 10.4 %collective-permute-start.4 = (f32[1,4,128]{2,1,0:T(4,128)S(1)}, f32[1,4,128]{2,1,0:T(4,128)S(1)}, u32[]{:S(2)}, u32[]{:S(2)}) collective-permute-start(f32[1,4,128]{2,1,0:T(4,128)S(1)} %bitcast.215), channel_id=1, source_target_pairs={{1,0},{2,1},{3,2},{4,3},{5,4},{6,5},{7,6},{8,7},{9,8},{10,9},{11,1... | collective-permute-start | bytes 6152 | tf_op jit(solution)/shard_map/ppermute | solution.py:29
  41.0 9.7 %copy-start.20 = (f32[7]{0:T(128)S(1)}, f32[7]{0:T(128)}, u32[]{:S(2)}) copy-start(f32[7]{0:T(128)} %constant.42.clone) | copy-start | bytes 88
  41.0 9.7 %copy-start.21 = (f32[7]{0:T(128)S(1)}, f32[7]{0:T(128)}, u32[]{:S(2)}) copy-start(f32[7]{0:T(128)} %constant.43.clone) | copy-start | bytes 88
  41.0 10.5 %collective-permute-start.5 = (f32[1,4,128]{2,1,0:T(4,128)S(1)}, f32[1,4,128]{2,1,0:T(4,128)S(1)}, u32[]{:S(2)}, u32[]{:S(2)}) collective-permute-start(f32[1,4,128]{2,1,0:T(4,128)S(1)} %bitcast.221), channel_id=1, source_target_pairs={{1,0},{2,1},{3,2},{4,3},{5,4},{6,5},{7,6},{8,7},{9,8},{10,9},{11,1... | collective-permute-start | bytes 6152 | tf_op jit(solution)/shard_map/ppermute | solution.py:29
  56.4 9.6 %copy-start.6 = (f32[22,22,1]{1,0,2:T(8,128)S(1)}, f32[22,22,1]{1,0,2:T(8,128)}, u32[]{:S(2)}) copy-start(f32[22,22,1]{1,0,2:T(8,128)} %constant.58) | copy-start | bytes 5812
  56.5 11.4 %collective-permute-start.6 = (f32[1,22,896]{2,0,1:T(1,128)S(1)}, f32[1,22,896]{2,0,1:T(1,128)S(1)}, u32[]{:S(2)}, u32[]{:S(2)}) collective-permute-start(f32[1,22,896]{2,0,1:T(1,128)S(1)} %slice.209), channel_id=1, source_target_pairs={{1,0},{2,1},{3,2},{4,3},{5,4},{6,5},{7,6},{8,7},{9,8},{10,9},{11,1... | collective-permute-start | bytes 236552 | tf_op jit(solution)/shard_map/ppermute | solution.py:17
  69.3 9.8 %collective-permute-start.7 = (f32[1,22,896]{2,0,1:T(1,128)S(1)}, f32[1,22,896]{2,0,1:T(1,128)S(1)}, u32[]{:S(2)}, u32[]{:S(2)}) collective-permute-start(f32[1,22,896]{2,0,1:T(1,128)S(1)} %slice.211), channel_id=1, source_target_pairs={{511,0},{0,1},{1,2},{2,3},{3,4},{4,5},{5,6},{6,7},{7,8},{8,9},{9,1... | collective-permute-start | bytes 236552 | tf_op jit(solution)/shard_map/ppermute | solution.py:17
  72.3 6.9 %copy-start.3 = (f32[7,896,22]{1,2,0:T(8,128)S(1)}, f32[7,896,22]{1,2,0:T(8,128)}, u32[]{:S(2)}) copy-start(f32[7,896,22]{1,2,0:T(8,128)} %fusion.46) | copy-start | bytes 1655812
  72.3 6.9 %copy-start.5 = (f32[7,22,896]{2,1,0:T(8,128)S(1)}, f32[7,22,896]{2,1,0:T(8,128)}, u32[]{:S(2)}) copy-start(f32[7,22,896]{2,1,0:T(8,128)} %reshape.159) | copy-start | bytes 1655812
  189.0 4.9 %collective-permute-start.8 = (f32[4,128]{1,0:T(4,128)S(1)}, f32[4,128]{1,0:T(4,128)S(1)}, u32[]{:S(2)}, u32[]{:S(2)}) collective-permute-start(f32[4,128]{1,0:T(4,128)S(1)} %bitcast.219), channel_id=1, source_target_pairs={{511,0},{0,1},{1,2},{2,3},{3,4},{4,5},{5,6},{6,7},{7,8},{8,9},{9,1... | collective-permute-start | bytes 6152 | tf_op jit(solution)/shard_map/ppermute | solution.py:17
  194.0 10.0 %collective-permute-start.10 = (f32[1,4,128]{2,1,0:T(4,128)S(1)}, f32[1,4,128]{2,1,0:T(4,128)S(1)}, u32[]{:S(2)}, u32[]{:S(2)}) collective-permute-start(f32[1,4,128]{2,1,0:T(4,128)S(1)} %bitcast.210), channel_id=1, source_target_pairs={{1,0},{2,1},{3,2},{4,3},{5,4},{6,5},{7,6},{8,7},{9,8},{10,9},{11,1... | collective-permute-start | bytes 6152 | tf_op jit(solution)/shard_map/ppermute | solution.py:29
  202.0 3.1 collective-permute-start.9
  205.1 11.3 %collective-permute-start.11 = (f32[1,4,128]{2,1,0:T(4,128)S(1)}, f32[1,4,128]{2,1,0:T(4,128)S(1)}, u32[]{:S(2)}, u32[]{:S(2)}) collective-permute-start(f32[1,4,128]{2,1,0:T(4,128)S(1)} %bitcast.212), channel_id=1, source_target_pairs={{0,1},{1,2},{2,3},{3,4},{4,5},{5,6},{6,7},{7,8},{8,9},{9,10},{10,1... | collective-permute-start | bytes 6152 | tf_op jit(solution)/shard_map/ppermute | solution.py:26
  208.9 8.2 %collective-permute-start.12 = (f32[1,4,128]{2,1,0:T(4,128)S(1)}, f32[1,4,128]{2,1,0:T(4,128)S(1)}, u32[]{:S(2)}, u32[]{:S(2)}) collective-permute-start(f32[1,4,128]{2,1,0:T(4,128)S(1)} %bitcast.213), channel_id=1, source_target_pairs={{1,0},{2,1},{3,2},{4,3},{5,4},{6,5},{7,6},{8,7},{9,8},{10,9},{11,1... | collective-permute-start | bytes 6152 | tf_op jit(solution)/shard_map/ppermute | solution.py:29
  217.2 10.4 %collective-permute-start.13 = (f32[1,4,128]{2,1,0:T(4,128)S(1)}, f32[1,4,128]{2,1,0:T(4,128)S(1)}, u32[]{:S(2)}, u32[]{:S(2)}) collective-permute-start(f32[1,4,128]{2,1,0:T(4,128)S(1)} %bitcast.220), channel_id=1, source_target_pairs={{1,0},{2,1},{3,2},{4,3},{5,4},{6,5},{7,6},{8,7},{9,8},{10,9},{11,1... | collective-permute-start | bytes 6152 | tf_op jit(solution)/shard_map/ppermute | solution.py:29
  348.0 5.7 %collective-permute-start.14 = (f32[1,22,896]{2,0,1:T(1,128)S(1)}, f32[1,22,896]{2,0,1:T(1,128)S(1)}, u32[]{:S(2)}, u32[]{:S(2)}) collective-permute-start(f32[1,22,896]{2,0,1:T(1,128)S(1)} %slice.223), channel_id=1, source_target_pairs={{1,0},{2,1},{3,2},{4,3},{5,4},{6,5},{7,6},{8,7},{9,8},{10,9},{11,1... | collective-permute-start | bytes 236552 | tf_op jit(solution)/shard_map/ppermute | solution.py:17
  354.5 5.0 %collective-permute-start.15 = (f32[1,22,896]{2,0,1:T(1,128)S(1)}, f32[1,22,896]{2,0,1:T(1,128)S(1)}, u32[]{:S(2)}, u32[]{:S(2)}) collective-permute-start(f32[1,22,896]{2,0,1:T(1,128)S(1)} %slice.225), channel_id=1, source_target_pairs={{511,0},{0,1},{1,2},{2,3},{3,4},{4,5},{5,6},{6,7},{7,8},{8,9},{9,1... | collective-permute-start | bytes 236552 | tf_op jit(solution)/shard_map/ppermute | solution.py:17
  (15 other events, 22.2 us)
where the time goes:
time: 469 us; the launch traced here: 468 us
  blocking collectives  318 us (68%)
  starting transfers between devices  90.3 us (19%)
  waiting for transfers between devices  17.3 us (4%)
  local copies, waits for them, and re-layouts  17 us (4%)
  matrix products  11 us (2%)
  other arithmetic  8.71 us (2%)
  between operations  5.21 us (1%)
    psum x2, blocking collectives, residual_dot(): return lax.psum(jnp.sum(first * second), ('grp', 'dev'))  216 us
    psum x1, blocking collectives, per_device(): lax.psum(jnp.sum(direction * operated), ('grp', 'dev'))  103 us
    ppermute x6, starting transfers between devices, with_halo(): lax.ppermute(lax.slice_in_dim(block, 0, width, axis=dim), axis, backward)  55 us
    ppermute x6, starting transfers between devices, from_behind(): return lax.ppermute(block, axis, route)  25.7 us
    ppermute x6, waiting for transfers between devices, from_behind(): return lax.ppermute(block, axis, route)  13 us
    ppermute x4, starting transfers between devices, with_halo(): lax.ppermute(lax.slice_in_dim(block, block.shape[dim] - width, None, axis...  9.54 us
  transfers between devices with their start and end apart: 16, of which 10 were waited for; matrix products, arithmetic and copies ran while one was open for 2% of the time, Pallas kernels for 0%

commit v1 on v0

v1 whole, which is shorter than its diff:
```python
import functools

import jax
import jax.numpy as jnp
import numpy as np
from jax import lax
from jax.experimental import pallas as pl
from jax.experimental.pallas import tpu as pltpu
from jax.sharding import Mesh
from jax.sharding import PartitionSpec as P

def legendre_seven(points):
    return (429.0 * points**7 - 693.0 * points**5 + 315.0 * points**3 - 35.0 * points) / 16.0


def pad_vector(vector, before, after):
    return np.concatenate([np.zeros(before), vector, np.zeros(after)])


def pad_matrix(matrix, before, after):
    width = matrix.shape[1]
    rows = np.concatenate([np.zeros((before, width)), matrix, np.zeros((after, width))], axis=0)
    height = rows.shape[0]
    return np.concatenate([np.zeros((height, before)), rows, np.zeros((height, after))], axis=1)


def diag_entries(matrix):
    return np.array([matrix[k, k] for k in range(matrix.shape[0])])


def diag_matrix(vector):
    count = vector.shape[0]
    return np.stack([pad_vector(np.array([vector[k]]), k, count - 1 - k) for k in range(count)])


def gll_tables():
    gll_nodes = np.array(
        [
            -1.0,
            -0.8717401485096066,
            -0.5917001814331423,
            -0.2092992179024789,
            0.2092992179024789,
            0.5917001814331423,
            0.8717401485096066,
            1.0,
        ]
    )
    values = legendre_seven(gll_nodes)
    weights = 2.0 / (56.0 * values * values)
    spacing = gll_nodes[:, None] - gll_nodes[None, :]
    distinct = np.abs(spacing) > 1e-12
    divisor = np.where(distinct, spacing, 1.0)
    derivative = np.where(distinct, values[:, None] / values[None, :] / divisor, 0.0)
    derivative = derivative + diag_matrix(np.array([-14.0, 0.0, 0.0, 0.0, 0.0, 0.0, 0.0, 14.0]))
    stiffness = derivative.T @ (weights[:, None] * derivative)
    return (gll_nodes, weights, stiffness)


CSWEEPS = 3
damping = 0.6
EY = 3
NY = 7 * EY + 1
PY = 24
LANES = 128
ROWS = 7 * PY
FULL = 8 * PY
AXES = ("x", "y", "z", "core")
GRID = {512: (4, 4, 16, 2)}
VMEM_BYTES = 24 * 1024 * 1024


class Tables:
    def __init__(self):
        nodes, w, K = gll_tables()
        self.K = K
        low = (1.0 - nodes) / 2.0
        high = (1.0 + nodes) / 2.0
        self.low, self.high = low, high
        mass = np.concatenate([[w[0] + w[7]], w[1:7]])
        kdiag = np.diag(K)
        stiff = np.concatenate([[kdiag[0] + kdiag[7]], kdiag[1:7]])
        self.mass, self.stiff = mass, stiff
        my = np.zeros(PY)
        Ky = np.zeros((PY, PY))
        interp = np.zeros((PY, EY + 1))
        q = np.zeros((EY + 1, EY + 1))
        for e in range(EY):
            my[7 * e : 7 * e + 8] += w
            Ky[7 * e : 7 * e + 8, 7 * e : 7 * e + 8] += K
            q[e : e + 2, e : e + 2] += np.array([[0.5, -0.5], [-0.5, 0.5]])
        for n in range(NY):
            e = min(n // 7, EY - 1)
            interp[n, e] = low[n - 7 * e]
            interp[n, e + 1] = high[n - 7 * e]
        self.my, self.interp = my, interp
        real = (np.arange(PY) < NY).astype(np.float64)
        cy = np.array([1.0] + [2.0] * (EY - 1) + [1.0])
        wxy = np.zeros((FULL, FULL))
        for i in range(8):
            for j in range(8):
                block = K[i, j] * np.diag(my)
                if i == j and i < 7:
                    block = block + mass[i] * Ky
                wxy[PY * i : PY * i + PY, PY * j : PY * j + PY] = block
        self.wxy = wxy[:ROWS]
        p1 = np.concatenate([my * stiff[i] + mass[i] * np.diag(Ky) + (1.0 - real) for i in range(7)])
        p2 = np.concatenate([my * mass[i] for i in range(7)])
        rest = np.zeros((8, ROWS))
        for i in range(7):
            rest[0:4, PY * i : PY * i + PY] = low[i] * interp.T
            rest[4:8, PY * i : PY * i + PY] = high[i] * interp.T
        self.rest = rest
        alpha = float(np.dot(K[7, :7], low[:7]))
        beta = float(np.dot(K[7, :7], high[:7]))
        prol = np.zeros((FULL + PY, 16))
        for i in range(8):
            prol[PY * i : PY * i + PY, 4:8] = low[i] * interp
            prol[PY * i : PY * i + PY, 8:12] = high[i] * interp
        prol[FULL:, 0:4] = my[:, None] * (alpha * interp)
        prol[FULL:, 4:8] = my[:, None] * (beta * interp)
        self.prol = prol
        wide = lambda v: np.repeat(np.asarray(v)[:, None], LANES, axis=1)
        self.col = np.concatenate([wide(p1), wide(p2), wide(my)], axis=0).astype(np.float32)
        self.coarse = np.concatenate([wide(cy), wide(4.0 * cy + 4.0 * np.diag(q))], axis=0).astype(np.float32)


def split(matrix):
    matrix = np.asarray(matrix, np.float32)
    top = matrix.astype(jnp.bfloat16)
    return np.stack([top, (matrix - top.astype(np.float32)).astype(jnp.bfloat16)])


def dot(a, b):
    return jnp.dot(a, b, preferred_element_type=jnp.float32)


def split_dot(m_ref, value):
    top = value.astype(jnp.bfloat16)
    rest = (value - top.astype(jnp.float32)).astype(jnp.bfloat16)
    return dot(m_ref[0], top) + (dot(m_ref[0], rest) + dot(m_ref[1], top))


def up_one(value):
    return pltpu.roll(value, LANES - 1, 1)


def down_one(value):
    return pltpu.roll(value, 1, 1)


def tile(j):
    return slice(LANES * j, LANES * j + LANES)


def plane_rows(i):
    return slice(PY * i, PY * i + PY)


def head(t, field, dinv_ref, screen4, first, rest_ref, my_rows, u_ref, msib_ref, xout_ref):
    seven = [None] * 7
    for j in range(7):
        for i in range(7):
            u = field[plane_rows(i), tile(j)] * dinv_ref[plane_rows(i), tile(j)]
            u_ref[plane_rows(i), tile(j)] = u
            term = float(t.K[7, i]) * u
            seven[j] = term if i == 0 else seven[j] + term
    for j in range(7):
        seven_plane = (my_rows * seven[j]) * float(t.mass[j])
        zero_plane = u_ref[0:PY, tile(j)]
        xout_ref[PY * j : PY * j + PY, :] = jnp.where(first, zero_plane, seven_plane)
        msib_ref[PY * j : PY * j + PY, :] = jnp.where(first, seven_plane, zero_plane)
    low = float(t.low[0]) * field[:, tile(0)]
    high = float(t.high[1]) * field[:, tile(1)]
    for i in range(1, 7):
        low = low + float(t.low[i]) * field[:, tile(i)]
    for i in range(2, 7):
        high = high + float(t.high[i]) * field[:, tile(i)]
    along_z = low + down_one(high)
    msib_ref[ROWS : ROWS + 8, :] = split_dot(rest_ref, along_z)
    msib_ref[ROWS + 8 : ROWS + 12, :] = screen4
    msib_ref[ROWS + 12 : ROWS + 16, :] = jnp.zeros_like(screen4)


def first_kernel(t, r_ref, s_ref, col_ref, rest_ref, rp_ref, u_ref, dinv_ref, sm_ref, msib_ref, xout_ref):
    first = lax.axis_index("core") == 0
    zero = jnp.zeros((8, 7 * LANES), jnp.float32)
    for i in range(7):
        rp_ref[PY * i + 16 : PY * i + PY, :] = zero
        sm_ref[PY * i + 16 : PY * i + PY, :] = zero
        rp_ref[PY * i : PY * i + NY, :] = r_ref[i]
        sm_ref[PY * i : PY * i + NY, :] = s_ref[i]
    screen4 = jnp.concatenate([sm_ref[7 * q : 7 * q + 1, 0:LANES] for q in range(EY + 1)], axis=0)
    my_rows = col_ref[2 * ROWS : 2 * ROWS + PY, :]
    for i in range(7):
        p1 = col_ref[PY * i : PY * i + PY, :]
        p2 = col_ref[ROWS + PY * i : ROWS + PY * i + PY, :]
        for j in range(7):
            sm = (p2 * float(t.mass[j])) * sm_ref[plane_rows(i), tile(j)]
            sm_ref[plane_rows(i), tile(j)] = sm
            diag = sm + float(t.mass[j]) * p1 + float(t.stiff[j]) * p2
            dinv_ref[plane_rows(i), tile(j)] = 1.0 / diag
    head(t, rp_ref, dinv_ref, screen4, first, rest_ref, my_rows, u_ref, msib_ref, xout_ref)


def coarse_solve(packs, coarse_ref, second):
    cy = coarse_ref[0:4, :]
    base = coarse_ref[4:8, :]
    zero_row = jnp.zeros((1, LANES), jnp.float32)
    rhs, gain, values = {}, {}, {}
    for v in range(1, 9):
        rhs[v] = packs[v][0:4] + packs[v - 1][4:8]
        gain[v] = damping / (4.0 * cy * packs[v][8:12] + base)
        values[v] = gain[v] * rhs[v]
    for sweep in range(1, CSWEEPS):
        new = {}
        for v in range(1 + sweep, 9 - sweep):
            c = values[v]
            sides = values[v - 1] + values[v + 1] + up_one(c) + down_one(c)
            walls = jnp.concatenate([zero_row, c[0:3]], axis=0) + jnp.concatenate([c[1:4], zero_row], axis=0)
            new[v] = (1.0 - damping) * c + gain[v] * (rhs[v] + cy * sides + 2.0 * walls)
        values = new
    picked = [jnp.where(second, values[v + 1], values[v]) for v in (3, 4, 5)]
    return jnp.concatenate(picked + [jnp.zeros((4, LANES), jnp.float32)], axis=0)


def tail(t, u_ref, sm_ref, col_ref, ag1_ref, recv_ref, ag2_ref, coarse_ref, prol_ref, wxy_ref, z_ref, w_ref, full_ref, second):
    packs = []
    order = [(2, 0, 32), (2, 0, 48), (2, 0, 0), (2, 0, 16), (1, 0, ROWS), (1, 1, ROWS), (2, 1, 0), (2, 1, 16), (2, 1, 32), (2, 1, 48)]
    for which, core, row in order:
        ref = ag1_ref if which == 1 else ag2_ref
        packs.append(ref[core, row : row + 12, :])
    c = coarse_solve(packs, coarse_ref, second)
    fine = split_dot(prol_ref, c)
    fine_up = up_one(fine)
    my_rows = col_ref[2 * ROWS : 2 * ROWS + PY, :]
    incoming = []
    for j in range(7):
        f = float(t.low[j]) * fine + float(t.high[j]) * fine_up if j else fine
        sib0, sib1 = ag1_ref[0, PY * j : PY * j + PY, :], ag1_ref[1, PY * j : PY * j + PY, :]
        outer = recv_ref[PY * j : PY * j + PY, :]
        zero_plane = jnp.where(second, outer, sib1)
        seven_plane = jnp.where(second, sib0, outer)
        full_ref[0:ROWS, tile(j)] = u_ref[:, tile(j)] + f[0:ROWS]
        full_ref[ROWS:FULL, tile(j)] = zero_plane + f[ROWS:FULL]
        own = u_ref[0:PY, tile(j)]
        incoming.append(seven_plane + float(t.mass[j]) * (f[FULL : FULL + PY] + float(t.K[7, 7]) * my_rows * (own + f[0:PY])))
    xy = split_dot(wxy_ref, full_ref[...])
    K = t.K
    for i in range(7):
        p2 = col_ref[ROWS + PY * i : ROWS + PY * i + PY, :]
        parts = [full_ref[plane_rows(i), tile(j)] for j in range(7)]
        parts.append(up_one(parts[0]))
        out = []
        for m in range(8):
            acc = float(K[m, 0]) * parts[0]
            for j in range(1, 8):
                acc = acc + float(K[m, j]) * parts[j]
            out.append(acc)
        out[0] = out[0] + down_one(out[7])
        for j in range(7):
            w = sm_ref[plane_rows(i), tile(j)] * parts[j] + p2 * out[j] + float(t.mass[j]) * xy[plane_rows(i), tile(j)]
            if i == 0:
                w = w + incoming[j]
            w_ref[plane_rows(i), tile(j)] = w
            z_ref[plane_rows(i), tile(j)] = parts[j]


def partial(a_ref, b_ref):
    total = None
    for i in range(7):
        for j in range(7):
            term = a_ref[plane_rows(i), tile(j)] * b_ref[plane_rows(i), tile(j)]
            total = term if total is None else total + term
    return total[0:8] + total[8:16] + total[16:24]


def second_kernel(t, rp_ref, u_ref, dinv_ref, sm_ref, col_ref, rest_ref, coarse_ref, prol_ref, wxy_ref, ag1_ref, recv_ref, ag2_ref,
                  z_ref, w_ref, u2_ref, msib_ref, xout_ref, sums_ref, full_ref):
    core = lax.axis_index("core")
    tail(t, u_ref, sm_ref, col_ref, ag1_ref, recv_ref, ag2_ref, coarse_ref, prol_ref, wxy_ref, z_ref, w_ref, full_ref, core == 1)
    screen4 = jnp.where(core == 1, ag1_ref[1, ROWS + 8 : ROWS + 12, :], ag1_ref[0, ROWS + 8 : ROWS + 12, :])
    my_rows = col_ref[2 * ROWS : 2 * ROWS + PY, :]
    head(t, w_ref, dinv_ref, screen4, core == 0, rest_ref, my_rows, u2_ref, msib_ref, xout_ref)
    sums_ref[0:8, :] = partial(rp_ref, z_ref)
    sums_ref[8:16, :] = partial(z_ref, w_ref)


def third_kernel(t, w_ref, u_ref, sm_ref, col_ref, coarse_ref, prol_ref, wxy_ref, ag1_ref, recv_ref, ag2_ref, sums_in_ref,
                 v_ref, y_ref, sums_ref, full_ref):
    core = lax.axis_index("core")
    tail(t, u_ref, sm_ref, col_ref, ag1_ref, recv_ref, ag2_ref, coarse_ref, prol_ref, wxy_ref, v_ref, y_ref, full_ref, core == 1)
    groups = [sums_in_ref[0:8, :], sums_in_ref[8:16, :], partial(w_ref, v_ref), partial(v_ref, y_ref)]
    lane = lax.broadcasted_iota(jnp.int32, (1, LANES), 1) // 32
    row = jnp.zeros((1, LANES), jnp.float32)
    for k in range(4):
        total = jnp.sum(groups[k], axis=0, keepdims=True)
        total = total + pltpu.roll(total, 64, 1)
        total = total + pltpu.roll(total, 32, 1)
        row = jnp.where(lane == k, total, row)
    for g in range(sums_ref.shape[0]):
        sums_ref[g] = row


def spread_kernel(got_ref, out_ref):
    total = got_ref[0]
    for g in range(1, got_ref.shape[0]):
        total = total + got_ref[g]
    for g in range(out_ref.shape[0]):
        out_ref[g] = total


def last_kernel(r_ref, z_ref, w_ref, v_ref, y_ref, got_ref, x_ref, res_ref):
    total = got_ref[0]
    for g in range(1, got_ref.shape[0]):
        total = total + got_ref[g]
    lane = lax.broadcasted_iota(jnp.int32, (1, LANES), 1) // 32
    rho, pi, sigma, tau = [jnp.sum(jnp.where(lane == k, total, 0.0), axis=1, keepdims=True) for k in range(4)]
    step0 = rho / pi
    rho1 = step0 * step0 * sigma - rho
    ratio = 1.0 + rho1 / rho
    step1 = rho1 / (ratio * ratio * pi - 2.0 * ratio * step0 * sigma + step0 * step0 * tau)
    a = step0 + step1 * ratio
    b = step1 * step0
    for i in range(7):
        rows = slice(PY * i, PY * i + NY)
        x_ref[i] = a * z_ref[rows, :] - b * v_ref[rows, :]
        res_ref[i] = r_ref[i] - a * w_ref[rows, :] + b * y_ref[rows, :]


def f32(*shape):
    return jax.ShapeDtypeStruct(shape, jnp.float32)


def call(kernel, outs, args, scratch=(), name=None):
    space = pl.BlockSpec(memory_space=pltpu.VMEM)
    return pl.pallas_call(
        kernel,
        out_shape=outs,
        in_specs=[space] * len(args),
        out_specs=[space] * len(outs) if isinstance(outs, (list, tuple)) else space,
        scratch_shapes=list(scratch),
        compiler_params=pltpu.CompilerParams(vmem_limit_bytes=VMEM_BYTES),
        name=name,
    )(*args)


def chip_permute(block, distance):
    count = 1
    for axis in AXES:
        count *= lax.axis_size(axis)
    chips = count // 2
    route = []
    for device in range(count):
        chip, core = divmod(device, 2)
        route.append((device, 2 * ((chip + distance) % chips) if core else 2 * ((chip - distance) % chips) + 1))
    return lax.ppermute(block, AXES, route)


def halo(msib, xout):
    ag1 = lax.all_gather(msib, "core")
    packs = ag1[:, ROWS:, :].reshape(32, LANES)
    far = chip_permute(packs, 2)
    near = chip_permute(jnp.concatenate([xout, packs], axis=0), 1)
    ag2 = lax.all_gather(jnp.concatenate([near[ROWS:], far], axis=0), "core")
    return ag1, near, ag2


def per_device(right_side, screening):
    t = Tables()
    col = jnp.asarray(t.col)
    coarse = jnp.asarray(t.coarse)
    rest, prol, wxy = (jnp.asarray(split(m)) for m in (t.rest, t.prol, t.wxy))
    big = f32(ROWS, 7 * LANES)
    msg = [f32(ROWS + 16, LANES), f32(ROWS, LANES)]
    rp, u, dinv, sm, msib, xout = call(
        functools.partial(first_kernel, t), [big] * 4 + msg, (right_side, screening, col, rest), name="first"
    )
    ag1, near, ag2 = halo(msib, xout)
    full = pltpu.VMEM((FULL, 7 * LANES), jnp.float32)
    z, w, u2, msib, xout, sums = call(
        functools.partial(second_kernel, t), [big] * 3 + msg + [f32(16, LANES)],
        (rp, u, dinv, sm, col, rest, coarse, prol, wxy, ag1, near, ag2), [full], name="second",
    )
    ag1, near, ag2 = halo(msib, xout)
    groups = lax.axis_size(("x", "y"))
    rest_count = lax.axis_size(("z", "core"))
    v, y, sums = call(
        functools.partial(third_kernel, t), [big, big, f32(groups, 1, LANES)],
        (w, u2, sm, col, coarse, prol, wxy, ag1, near, ag2, sums), [full], name="third",
    )
    got = lax.all_to_all(sums, ("x", "y"), 0, 0, tiled=True)
    sums = call(spread_kernel, f32(rest_count, 1, LANES), (got,), name="spread")
    got = lax.all_to_all(sums, ("z", "core"), 0, 0, tiled=True)
    return call(last_kernel, [f32(*right_side.shape)] * 2, (right_side, z, w, v, y, got), name="last")


def solution(mesh):
    devices = np.asarray(mesh.devices)
    shape = GRID.get(devices.size) or (1, 1, devices.size // 2, 2)
    fine_mesh = Mesh(devices.reshape(shape), AXES)
    spec = P(AXES, None, None)
    return jax.shard_map(per_device, mesh=fine_mesh, in_specs=(spec, spec), out_specs=(spec, spec), check_vma=False)
```

time: 469 us -> 90.1 us (0.19)
  blocking collectives: 318 us -> 63.5 us
  starting transfers between devices: 90.3 us -> 7.81 us
  local copies, waits for them, and re-layouts: 17 us -> 4.45 us
  matrix products: 11 us -> 0 us
  waiting for transfers between devices: 17.3 us -> 8.05 us
  other arithmetic: 8.71 us -> 0.02 us
  Pallas kernels: 0 us -> 4.99 us
    psum x3 -> x0, blocking collectives: 318 us -> none  [the longest x2 216 us: residual_dot(): return lax.psum(jnp.sum(first * second), ('grp', 'dev'))]
    ppermute x16 -> x4, starting transfers between devices: 90.3 us -> 7.81 us  [chip_permute(): return lax.ppermute(block, AXES, route)]
    all_gather x0 -> x4, blocking collectives: none -> 33.6 us  [the longest x2 23.1 us: halo(): ag2 = lax.all_gather(jnp.concatenate([near[ROWS:], far], axis=0), 'core')]
    all_to_all x0 -> x2, blocking collectives: none -> 29.9 us  [the longest x1 20.9 us: per_device(): got = lax.all_to_all(sums, ('z', 'core'), 0, 0, tiled=True)]
    dot_general x22 -> x0, matrix products: 11 us -> none  [the longest x2 3.08 us: stiff_along_y(): jnp.einsum('mn,xnz->xmz', stiff_y, grid_values, precision=lax.Precision.H...]
    ppermute x16 -> x4, waiting for transfers between devices: 17.3 us -> 8.05 us  [chip_permute(): return lax.ppermute(block, AXES, route)]
    reduce_sum x3 -> x0, other arithmetic: 5.23 us -> none  [the longest x1 2.63 us: residual_dot(): return lax.psum(jnp.sum(first * second), ('grp', 'dev'))]
    pallas_call x0 -> x5, Pallas kernels: none -> 4.99 us  [call(): pl.pallas_call(kernel, out_shape=outs, in_specs=[space] * len(args), out_...]
  transfers between devices with their start and end apart: 16 -> 4, of which waited for: 10 -> 4; matrix products, arithmetic and copies ran while one was open for 2% -> 0% of each run, Pallas kernels for 0% -> 0%
where the time goes in v1:
time: 90.1 us; the launch traced here: 89.5 us
  blocking collectives  63.5 us (70%)
  waiting for transfers between devices  8.05 us (9%)
  starting transfers between devices  7.81 us (9%)
  Pallas kernels  4.99 us (6%)
  local copies, waits for them, and re-layouts  4.45 us (5%)
    all_gather x2, blocking collectives, halo(): ag2 = lax.all_gather(jnp.concatenate([near[ROWS:], far], axis=0), 'core')  23.1 us
    all_to_all x1, blocking collectives, per_device(): got = lax.all_to_all(sums, ('z', 'core'), 0, 0, tiled=True)  20.9 us
    all_gather x2, blocking collectives, halo(): ag1 = lax.all_gather(msib, 'core')  10.6 us
    all_to_all x1, blocking collectives, per_device(): got = lax.all_to_all(sums, ('x', 'y'), 0, 0, tiled=True)  8.95 us
    ppermute x4, waiting for transfers between devices, chip_permute(): return lax.ppermute(block, AXES, route)  8.05 us
    ppermute x4, starting transfers between devices, chip_permute(): return lax.ppermute(block, AXES, route)  7.81 us
    pallas_call x5, Pallas kernels, call(): pl.pallas_call(kernel, out_shape=outs, in_specs=[space] * len(args), out_...  4.99 us
    unnamed x18, local copies, waits for them, and re-layouts  4.44 us
  transfers between devices with their start and end apart: 4, of which 4 were waited for; matrix products, arithmetic and copies ran while one was open for 0% of the time, Pallas kernels for 0%

profile of v1, /device:TPU:1, one launch (start us, length us, event | category | flops | bytes accessed | tf_op | source)
XLA Modules:
  0.0 89.5 jit_solution(2166138224517342627)
XLA Ops:
  0.6 0.0 copy-start
  0.6 1.1 %copy-done = f32[7,22,896]{2,1,0:T(8,128)S(1)} copy-done((f32[7,22,896]{2,1,0:T(8,128)S(1)}, f32[7,22,896]{2,1,0:T(8,128)}, u32[]{:S(2)}) %copy-start) | copy-done | bytes 551960
  1.7 0.9 %copy-done.2 = f32[360,128]{1,0:T(8,128)S(1)} copy-done((f32[360,128]{1,0:T(8,128)S(1)}, f32[360,128]{1,0:T(8,128)}, u32[]{:S(2)}) %copy-start.2) | copy-done | bytes 184344
  2.6 1.1 %copy-done.5 = f32[7,22,896]{2,1,0:T(8,128)S(1)} copy-done((f32[7,22,896]{2,1,0:T(8,128)S(1)}, f32[7,22,896]{2,1,0:T(8,128)}, u32[]{:S(2)}) %copy-start.5) | copy-done | bytes 551960
  3.7 0.7 copy-done.7
  4.4 0.4 first.1
  4.8 8.6 %all-gather = f32[368,128]{1,0:T(8,128)S(1)} all-gather(f32[184,128]{1,0:T(8,128)S(1)} %get-tuple-element.21), channel_id=2, replica_groups=mesh['x'=4,'y'=4,'z'=16,'core'=2] {'core'}, dimensions={0}, use_global_device_ids=true | all-gather | bytes 282624 | tf_op jit(solution)/shard_map/all_gather | solution.py:361
  13.5 2.1 %collective-permute-start = (f32[200,128]{1,0:T(8,128)S(1)}, f32[200,128]{1,0:T(8,128)S(1)}, u32[]{:S(2)}, u32[]{:S(2)}) collective-permute-start(f32[200,128]{1,0:T(8,128)S(1)} %pad_maximum_fusion), channel_id=1, source_target_pairs={{0,511},{1,2},{2,1},{3,4},{4,3},{5,6},{6,5},{7,8},{8,7},{9,10},{10... | collective-permute-start | bytes 307208 | tf_op jit(solution)/shard_map/ppermute | solution.py:357
  15.5 1.9 %collective-permute-start.1 = (f32[32,128]{1,0:T(8,128)S(1)}, f32[32,128]{1,0:T(8,128)S(1)}, u32[]{:S(2)}, u32[]{:S(2)}) collective-permute-start(f32[32,128]{1,0:T(8,128)S(1)} %bitcast.13), channel_id=1, source_target_pairs={{0,509},{1,4},{2,511},{3,6},{4,1},{5,8},{6,3},{7,10},{8,5},{9,12},... | collective-permute-start | bytes 49160 | tf_op jit(solution)/shard_map/ppermute | solution.py:357
  17.5 2.1 %collective-permute-done.recv_ref = f32[200,128]{1,0:T(8,128)S(1)} collective-permute-done((f32[200,128]{1,0:T(8,128)S(1)}, f32[200,128]{1,0:T(8,128)S(1)}, u32[]{:S(2)}, u32[]{:S(2)}) %collective-permute-start) | collective-permute-done | bytes 102432 | tf_op jit(solution)/shard_map/ppermute | solution.py:357
  19.6 1.9 %collective-permute-done.1 = f32[32,128]{1,0:T(8,128)S(1)} collective-permute-done((f32[32,128]{1,0:T(8,128)S(1)}, f32[32,128]{1,0:T(8,128)S(1)}, u32[]{:S(2)}, u32[]{:S(2)}) %collective-permute-start.1) | collective-permute-done | bytes 16416 | tf_op jit(solution)/shard_map/ppermute | solution.py:357
  21.5 15.8 %all-gather.1 = f32[128,128]{1,0:T(8,128)S(1)} all-gather(f32[64,128]{1,0:T(8,128)S(1)} %pad_maximum_fusion.2), channel_id=3, replica_groups=mesh['x'=4,'y'=4,'z'=16,'core'=2] {'core'}, dimensions={0}, use_global_device_ids=true | all-gather | bytes 98304 | tf_op jit(solution)/shard_map/all_gather | solution.py:365
  37.3 0.7 copy-done.8
  38.0 1.7 %second.1 = (f32[168,896]{1,0:T(8,128)S(1)}, f32[168,896]{1,0:T(8,128)S(1)}, f32[168,896]{1,0:T(8,128)S(1)}, f32[184,128]{1,0:T(8,128)S(1)}, f32[168,128]{1,0:T(8,128)S(1)}, /*index=5*/f32[16,128]{1,0:T(8,128)S(1)}) custom-call(f32[168,896]{1,0:T(8,128)S(1)} %get-tuple-element.17.rp_ref, f32[168,896]{1,0:T(8,128)S(1)} %get-tuple-element.18.u_ref, ...), custom_call_target="tpu_custom_call" | custom-call | tf_op jit(solution)/shard_map/second/pallas_call | solution.py:337
  39.7 1.9 %all-gather.2 = f32[368,128]{1,0:T(8,128)S(1)} all-gather(f32[184,128]{1,0:T(8,128)S(1)} %get-tuple-element.26), channel_id=4, replica_groups=mesh['x'=4,'y'=4,'z'=16,'core'=2] {'core'}, dimensions={0}, use_global_device_ids=true | all-gather | bytes 282624 | tf_op jit(solution)/shard_map/all_gather | solution.py:361
  41.6 1.9 %collective-permute-start.2 = (f32[200,128]{1,0:T(8,128)S(1)}, f32[200,128]{1,0:T(8,128)S(1)}, u32[]{:S(2)}, u32[]{:S(2)}) collective-permute-start(f32[200,128]{1,0:T(8,128)S(1)} %pad_maximum_fusion.1), channel_id=1, source_target_pairs={{0,511},{1,2},{2,1},{3,4},{4,3},{5,6},{6,5},{7,8},{8,7},{9,10},{10... | collective-permute-start | bytes 307208 | tf_op jit(solution)/shard_map/ppermute | solution.py:357
  43.6 1.9 %collective-permute-start.3 = (f32[32,128]{1,0:T(8,128)S(1)}, f32[32,128]{1,0:T(8,128)S(1)}, u32[]{:S(2)}, u32[]{:S(2)}) collective-permute-start(f32[32,128]{1,0:T(8,128)S(1)} %bitcast.15), channel_id=1, source_target_pairs={{0,509},{1,4},{2,511},{3,6},{4,1},{5,8},{6,3},{7,10},{8,5},{9,12},... | collective-permute-start | bytes 49160 | tf_op jit(solution)/shard_map/ppermute | solution.py:357
  45.5 2.1 %collective-permute-done.2.recv_ref = f32[200,128]{1,0:T(8,128)S(1)} collective-permute-done((f32[200,128]{1,0:T(8,128)S(1)}, f32[200,128]{1,0:T(8,128)S(1)}, u32[]{:S(2)}, u32[]{:S(2)}) %collective-permute-start.2) | collective-permute-done | bytes 102432 | tf_op jit(solution)/shard_map/ppermute | solution.py:357
  47.6 1.9 %collective-permute-done.3 = f32[32,128]{1,0:T(8,128)S(1)} collective-permute-done((f32[32,128]{1,0:T(8,128)S(1)}, f32[32,128]{1,0:T(8,128)S(1)}, u32[]{:S(2)}, u32[]{:S(2)}) %collective-permute-start.3) | collective-permute-done | bytes 16416 | tf_op jit(solution)/shard_map/ppermute | solution.py:357
  49.5 7.3 %all-gather.3 = f32[128,128]{1,0:T(8,128)S(1)} all-gather(f32[64,128]{1,0:T(8,128)S(1)} %pad_maximum_fusion.3), channel_id=5, replica_groups=mesh['x'=4,'y'=4,'z'=16,'core'=2] {'core'}, dimensions={0}, use_global_device_ids=true | all-gather | bytes 98304 | tf_op jit(solution)/shard_map/all_gather | solution.py:365
  56.8 1.5 %third.1 = (f32[168,896]{1,0:T(8,128)S(1)}, f32[168,896]{1,0:T(8,128)S(1)}, f32[16,1,128]{2,1,0:T(1,128)S(1)}) custom-call(f32[168,896]{1,0:T(8,128)S(1)} %get-tuple-element.24.w_ref, f32[168,896]{1,0:T(8,128)S(1)} %get-tuple-element.25.u_ref, f32[168,896]{1,0:T(8,128)S(1)} %get-tuple-element.20.sm_ref, f32[360,128]{1,0:T(8,128)S(1)} %copy-done.3, ...), custom_call_target="tpu_custom_call" | custom-call | tf_op jit(solution)/shard_map/third/pallas_call | solution.py:337
  58.3 9.0 %all_to_all.10.got_ref = f32[16,1,128]{2,1,0:T(1,128)S(1)} all-to-all(f32[16,1,128]{2,1,0:T(1,128)S(1)} %get-tuple-element.31), channel_id=1, replica_groups=mesh['x'=4,'y'=4,'z'=16,'core'=2] {'x','y'}, dimensions={0} | all-to-all | bytes 16384 | tf_op jit(solution)/shard_map/all_to_all | solution.py:392
  67.3 20.9 %all_to_all.11.got_ref = f32[32,1,128]{2,1,0:T(1,128)S(1)} all-to-all(f32[32,1,128]{2,1,0:T(1,128)S(1)} %spread.1), channel_id=1, replica_groups=mesh['x'=4,'y'=4,'z'=16,'core'=2] {'z','core'}, dimensions={0} | all-to-all | bytes 32768 | tf_op jit(solution)/shard_map/all_to_all | solution.py:394
  88.2 1.3 %last.1 = (f32[7,22,896]{2,1,0:T(8,128)}, f32[7,22,896]{2,1,0:T(8,128)}) custom-call(f32[7,22,896]{2,1,0:T(8,128)S(1)} %copy-done.1, f32[168,896]{1,0:T(8,128)S(1)} %get-tuple-element.23.z_ref, f32[168,896]{1,0:T(8,128)S(1)} %get-tuple-element.24.w_ref, f32[168,896]{1,0:T(8,128)S(1)} %get-tuple-element.29.v_ref, f32[168,896]{1,0:T(8,128)S(1)} %get-tuple-element.30.y_ref, ...), custom_call_target="tpu_custom_call" | custom-call | tf_op jit(solution)/shard_map/last/pallas_call | solution.py:337
  (21 shorter events, 0.1 us)
Async XLA Ops:
  0.6 1.1 %copy-start = (f32[7,22,896]{2,1,0:T(8,128)S(1)}, f32[7,22,896]{2,1,0:T(8,128)}, u32[]{:S(2)}) copy-start(f32[7,22,896]{2,1,0:T(8,128)} %r_ref.3) | copy-start | bytes 1655812
  1.7 0.9 %copy-start.2 = (f32[360,128]{1,0:T(8,128)S(1)}, f32[360,128]{1,0:T(8,128)}, u32[]{:S(2)}) copy-start(f32[360,128]{1,0:T(8,128)} %constant.10.clone.col_ref) | copy-start | bytes 552964
  2.6 1.1 %copy-start.5 = (f32[7,22,896]{2,1,0:T(8,128)S(1)}, f32[7,22,896]{2,1,0:T(8,128)}, u32[]{:S(2)}) copy-start(f32[7,22,896]{2,1,0:T(8,128)} %s_ref.1) | copy-start | bytes 1655812
  3.7 0.7 copy-start.7
  4.8 32.5 %copy-start.6 = (bf16[2,216,16]{2,1,0:T(8,128)(2,1)S(1)}, bf16[2,216,16]{2,1,0:T(8,128)(2,1)}, u32[]{:S(2)}) copy-start(bf16[2,216,16]{2,1,0:T(8,128)(2,1)} %constant.13.clone.prol_ref) | copy-start | bytes 41476
  13.5 23.8 %copy-start.3 = (f32[360,128]{1,0:T(8,128)S(1)}, f32[360,128]{1,0:T(8,128)}, u32[]{:S(2)}) copy-start(f32[360,128]{1,0:T(8,128)} %constant.10.clone.col_ref) | copy-start | bytes 552964
  13.5 23.8 %copy-start.4 = (bf16[2,168,192]{2,1,0:T(8,128)(2,1)S(1)}, bf16[2,168,192]{2,1,0:T(8,128)(2,1)}, u32[]{:S(2)}) copy-start(bf16[2,168,192]{2,1,0:T(8,128)(2,1)} %constant.14.clone.wxy_ref) | copy-start | bytes 387076
  13.5 6.1 %collective-permute-start = (f32[200,128]{1,0:T(8,128)S(1)}, f32[200,128]{1,0:T(8,128)S(1)}, u32[]{:S(2)}, u32[]{:S(2)}) collective-permute-start(f32[200,128]{1,0:T(8,128)S(1)} %pad_maximum_fusion), channel_id=1, source_target_pairs={{0,511},{1,2},{2,1},{3,4},{4,3},{5,6},{6,5},{7,8},{8,7},{9,10},{10... | collective-permute-start | bytes 307208 | tf_op jit(solution)/shard_map/ppermute | solution.py:357
  15.5 6.0 %collective-permute-start.1 = (f32[32,128]{1,0:T(8,128)S(1)}, f32[32,128]{1,0:T(8,128)S(1)}, u32[]{:S(2)}, u32[]{:S(2)}) collective-permute-start(f32[32,128]{1,0:T(8,128)S(1)} %bitcast.13), channel_id=1, source_target_pairs={{0,509},{1,4},{2,511},{3,6},{4,1},{5,8},{6,3},{7,10},{8,5},{9,12},... | collective-permute-start | bytes 49160 | tf_op jit(solution)/shard_map/ppermute | solution.py:357
  37.3 0.7 copy-start.8
  41.6 6.0 %collective-permute-start.2 = (f32[200,128]{1,0:T(8,128)S(1)}, f32[200,128]{1,0:T(8,128)S(1)}, u32[]{:S(2)}, u32[]{:S(2)}) collective-permute-start(f32[200,128]{1,0:T(8,128)S(1)} %pad_maximum_fusion.1), channel_id=1, source_target_pairs={{0,511},{1,2},{2,1},{3,4},{4,3},{5,6},{6,5},{7,8},{8,7},{9,10},{10... | collective-permute-start | bytes 307208 | tf_op jit(solution)/shard_map/ppermute | solution.py:357
  43.6 6.0 %collective-permute-start.3 = (f32[32,128]{1,0:T(8,128)S(1)}, f32[32,128]{1,0:T(8,128)S(1)}, u32[]{:S(2)}, u32[]{:S(2)}) collective-permute-start(f32[32,128]{1,0:T(8,128)S(1)} %bitcast.15), channel_id=1, source_target_pairs={{0,509},{1,4},{2,511},{3,6},{4,1},{5,8},{6,3},{7,10},{8,5},{9,12},... | collective-permute-start | bytes 49160 | tf_op jit(solution)/shard_map/ppermute | solution.py:357
  56.8 31.4 %copy-start.1 = (f32[7,22,896]{2,1,0:T(8,128)S(1)}, f32[7,22,896]{2,1,0:T(8,128)}, u32[]{:S(2)}) copy-start(f32[7,22,896]{2,1,0:T(8,128)} %r_ref.3) | copy-start | bytes 1655812

commit v2 on v1

v2 whole, which is shorter than its diff:
```python
import functools

import jax
import jax.numpy as jnp
import numpy as np
from jax import lax
from jax.experimental import pallas as pl
from jax.experimental.pallas import tpu as pltpu
from jax.sharding import Mesh
from jax.sharding import PartitionSpec as P

def legendre_seven(points):
    return (429.0 * points**7 - 693.0 * points**5 + 315.0 * points**3 - 35.0 * points) / 16.0


def pad_vector(vector, before, after):
    return np.concatenate([np.zeros(before), vector, np.zeros(after)])


def pad_matrix(matrix, before, after):
    width = matrix.shape[1]
    rows = np.concatenate([np.zeros((before, width)), matrix, np.zeros((after, width))], axis=0)
    height = rows.shape[0]
    return np.concatenate([np.zeros((height, before)), rows, np.zeros((height, after))], axis=1)


def diag_entries(matrix):
    return np.array([matrix[k, k] for k in range(matrix.shape[0])])


def diag_matrix(vector):
    count = vector.shape[0]
    return np.stack([pad_vector(np.array([vector[k]]), k, count - 1 - k) for k in range(count)])


def gll_tables():
    gll_nodes = np.array(
        [
            -1.0,
            -0.8717401485096066,
            -0.5917001814331423,
            -0.2092992179024789,
            0.2092992179024789,
            0.5917001814331423,
            0.8717401485096066,
            1.0,
        ]
    )
    values = legendre_seven(gll_nodes)
    weights = 2.0 / (56.0 * values * values)
    spacing = gll_nodes[:, None] - gll_nodes[None, :]
    distinct = np.abs(spacing) > 1e-12
    divisor = np.where(distinct, spacing, 1.0)
    derivative = np.where(distinct, values[:, None] / values[None, :] / divisor, 0.0)
    derivative = derivative + diag_matrix(np.array([-14.0, 0.0, 0.0, 0.0, 0.0, 0.0, 0.0, 14.0]))
    stiffness = derivative.T @ (weights[:, None] * derivative)
    return (gll_nodes, weights, stiffness)


CSWEEPS = 3
damping = 0.6
EY = 3
NY = 7 * EY + 1
PY = 24
LANES = 128
ROWS = 7 * PY
AXES = ("x", "y", "z", "core")
GRID = {512: (4, 4, 16, 2)}
VMEM_BYTES = 24 * 1024 * 1024
WIDE_VMEM_BYTES = 54784 * 1024
SIDE_FLOPS = 500_000_000


class Tables:
    def __init__(self):
        nodes, w, K = gll_tables()
        self.K = K
        low = (1.0 - nodes) / 2.0
        high = (1.0 + nodes) / 2.0
        self.low, self.high = low, high
        mass = np.concatenate([[w[0] + w[7]], w[1:7]])
        kdiag = np.diag(K)
        stiff = np.concatenate([[kdiag[0] + kdiag[7]], kdiag[1:7]])
        self.mass, self.stiff = mass, stiff
        my = np.zeros(PY)
        Ky = np.zeros((PY, PY))
        interp = np.zeros((PY, EY + 1))
        q = np.zeros((EY + 1, EY + 1))
        for e in range(EY):
            my[7 * e : 7 * e + 8] += w
            Ky[7 * e : 7 * e + 8, 7 * e : 7 * e + 8] += K
            q[e : e + 2, e : e + 2] += np.array([[0.5, -0.5], [-0.5, 0.5]])
        for n in range(NY):
            e = min(n // 7, EY - 1)
            interp[n, e] = low[n - 7 * e]
            interp[n, e + 1] = high[n - 7 * e]
        self.my, self.interp = my, interp
        real = (np.arange(PY) < NY).astype(np.float64)
        cy = np.array([1.0] + [2.0] * (EY - 1) + [1.0])
        wxy = np.zeros((ROWS, ROWS))
        for i in range(7):
            for j in range(7):
                block = K[i, j] * np.diag(my)
                if i == j:
                    block = block + mass[i] * Ky
                    if i == 0:
                        block = block + K[7, 7] * np.diag(my)
                wxy[PY * i : PY * i + PY, PY * j : PY * j + PY] = block
        self.wxy = wxy
        prol = np.zeros((2 * ROWS, 16))
        for i in range(7):
            prol[PY * i : PY * i + PY, 4:8] = low[i] * interp
            prol[PY * i : PY * i + PY, 8:12] = high[i] * interp
            rows = slice(ROWS + PY * i, ROWS + PY * i + PY)
            prol[rows, 4:8] = mass[i] * low[i] * (Ky @ interp)
            prol[rows, 8:12] = mass[i] * high[i] * (Ky @ interp)
        rows = slice(ROWS, ROWS + PY)
        prol[rows, 0:4] -= 0.5 * my[:, None] * interp
        prol[rows, 4:8] += my[:, None] * interp
        prol[rows, 8:12] -= 0.5 * my[:, None] * interp
        self.prol = prol
        wide = lambda v: np.repeat(np.asarray(v)[:, None], LANES, axis=1)
        self.rows = [my, np.diag(Ky), 1.0 - real] + [interp[:, k] for k in range(EY + 1)]
        tables = [wide(v) for v in self.rows] + [wide(cy), wide(4.0 * cy + 4.0 * np.diag(q))]
        self.col = np.concatenate(tables, axis=0).astype(np.float32)


def split(matrix):
    matrix = np.asarray(matrix, np.float32)
    top = matrix.astype(jnp.bfloat16)
    return np.stack([top, (matrix - top.astype(np.float32)).astype(jnp.bfloat16)])


def dot(a, b):
    return jnp.dot(a, b, preferred_element_type=jnp.float32)


def split_dot(m_ref, value):
    top = value.astype(jnp.bfloat16)
    rest = (value - top.astype(jnp.float32)).astype(jnp.bfloat16)
    return dot(m_ref[0], top) + (dot(m_ref[0], rest) + dot(m_ref[1], top))


def up_one(value):
    return pltpu.roll(value, LANES - 1, 1)


def down_one(value):
    return pltpu.roll(value, 1, 1)


def tile(j):
    return slice(LANES * j, LANES * j + LANES)


def plane_rows(i):
    return slice(PY * i, PY * i + PY)


def row_table(values):
    row = lax.broadcasted_iota(jnp.int32, (PY, LANES), 0)
    out = jnp.zeros((PY, LANES), jnp.float32)
    for n, value in enumerate(values):
        if value:
            out = jnp.where(row == n, float(value), out)
    return out


def row_tables(col_ref):
    return [col_ref[PY * k : PY * k + PY, :] for k in range(EY + 4)]


def head(t, field, dinv_ref, screen4, first, rows, u_ref, msib_ref, xout_ref):
    seven = [None] * 7
    for j in range(7):
        for i in range(7):
            u = field[plane_rows(i), tile(j)] * dinv_ref[plane_rows(i), tile(j)]
            u_ref[plane_rows(i), tile(j)] = u
            term = float(t.K[7, i]) * u
            seven[j] = term if i == 0 else seven[j] + term
    for j in range(7):
        seven_plane = (rows[0] * seven[j]) * float(t.mass[j])
        zero_plane = u_ref[0:PY, tile(j)]
        xout_ref[PY * j : PY * j + PY, :] = jnp.where(first, zero_plane, seven_plane)
        msib_ref[PY * j : PY * j + PY, :] = jnp.where(first, seven_plane, zero_plane)
    low = float(t.low[0]) * field[:, tile(0)]
    high = float(t.high[1]) * field[:, tile(1)]
    for i in range(1, 7):
        low = low + float(t.low[i]) * field[:, tile(i)]
    for i in range(2, 7):
        high = high + float(t.high[i]) * field[:, tile(i)]
    along_z = low + down_one(high)
    shares = [None, None]
    for i in range(7):
        for k, weight in enumerate((float(t.low[i]), float(t.high[i]))):
            if weight:
                term = weight * along_z[plane_rows(i)]
                shares[k] = term if shares[k] is None else shares[k] + term
    for k in range(2):
        for q in range(EY + 1):
            msib_ref[ROWS + 4 * k + q : ROWS + 4 * k + q + 1, :] = jnp.sum(shares[k] * rows[3 + q], axis=0, keepdims=True)
    msib_ref[ROWS + 8 : ROWS + 12, :] = screen4
    msib_ref[ROWS + 12 : ROWS + 16, :] = jnp.zeros_like(screen4)


def diagonal(t, s_ref, rows, dinv_ref, sm_ref):
    my_rows, ky_rows, pad_rows = rows[:3]
    zero = jnp.zeros((8, 7 * LANES), jnp.float32)
    for i in range(7):
        sm_ref[PY * i + 16 : PY * i + PY, :] = zero
        sm_ref[PY * i : PY * i + NY, :] = s_ref[i]
    screen4 = jnp.concatenate([sm_ref[7 * q : 7 * q + 1, 0:LANES] for q in range(EY + 1)], axis=0)
    for i in range(7):
        p1 = float(t.stiff[i]) * my_rows + float(t.mass[i]) * ky_rows + pad_rows
        p2 = float(t.mass[i]) * my_rows
        for j in range(7):
            sm = (p2 * float(t.mass[j])) * sm_ref[plane_rows(i), tile(j)]
            sm_ref[plane_rows(i), tile(j)] = sm
            diag = sm + float(t.mass[j]) * p1 + float(t.stiff[j]) * p2
            dinv_ref[plane_rows(i), tile(j)] = 1.0 / diag
    return screen4


def pad_planes(r_ref, rp_ref):
    zero = jnp.zeros((8, 7 * LANES), jnp.float32)
    for i in range(7):
        rp_ref[PY * i + 16 : PY * i + PY, :] = zero
        rp_ref[PY * i : PY * i + NY, :] = r_ref[i]


def first_kernel(t, r_hbm, s_hbm, msib_ref, xout_ref, r_ref, s_ref, rp_ref, u_ref, dinv_ref, sm_ref, sems):
    copies = [pltpu.make_async_copy(s_hbm, s_ref, sems.at[0]), pltpu.make_async_copy(r_hbm, r_ref, sems.at[1])]
    for copy in copies:
        copy.start()
    first = lax.axis_index("core") == 0
    rows = [row_table(v) for v in t.rows]
    copies[0].wait()
    screen4 = diagonal(t, s_ref, rows, dinv_ref, sm_ref)
    copies[1].wait()
    pad_planes(r_ref, rp_ref)
    head(t, rp_ref, dinv_ref, screen4, first, rows, u_ref, msib_ref, xout_ref)


def side_kernel(t, r_ref, s_ref, col_ref, wxy_ref, rp_ref, u_ref, dinv_ref, sm_ref, au_ref):
    diagonal(t, s_ref, row_tables(col_ref), dinv_ref, sm_ref)
    pad_planes(r_ref, rp_ref)
    for i in range(7):
        for j in range(7):
            u_ref[plane_rows(i), tile(j)] = rp_ref[plane_rows(i), tile(j)] * dinv_ref[plane_rows(i), tile(j)]
    apply_local(t, u_ref, sm_ref, col_ref, wxy_ref, au_ref)


def apply_local(t, u_ref, sm_ref, col_ref, wxy_ref, au_ref):
    xy = split_dot(wxy_ref, u_ref[...])
    my_rows = col_ref[0:PY, :]
    K = t.K
    for i in range(7):
        p2 = float(t.mass[i]) * my_rows
        parts = [u_ref[plane_rows(i), tile(j)] for j in range(7)]
        parts.append(up_one(parts[0]))
        out = []
        for m in range(8):
            acc = float(K[m, 0]) * parts[0]
            for j in range(1, 8):
                acc = acc + float(K[m, j]) * parts[j]
            out.append(acc)
        out[0] = out[0] + down_one(out[7])
        for j in range(7):
            au_ref[plane_rows(i), tile(j)] = (
                sm_ref[plane_rows(i), tile(j)] * parts[j] + p2 * out[j] + float(t.mass[j]) * xy[plane_rows(i), tile(j)]
            )


def partial(a_ref, b_ref):
    total = None
    for i in range(7):
        for j in range(7):
            term = a_ref[plane_rows(i), tile(j)] * b_ref[plane_rows(i), tile(j)]
            total = term if total is None else total + term
    return total[0:8] + total[8:16] + total[16:24]


def side_sums_kernel(t, u_ref, sm_ref, col_ref, wxy_ref, rp_ref, z_ref, w_ref, au_ref, sums_ref):
    apply_local(t, u_ref, sm_ref, col_ref, wxy_ref, au_ref)
    sums_ref[0:8, :] = partial(rp_ref, z_ref)
    sums_ref[8:16, :] = partial(z_ref, w_ref)


def coarse_solve(packs, coarse_ref, second):
    cy = coarse_ref[7 * PY : 7 * PY + 4, :]
    base = coarse_ref[7 * PY + 4 : 7 * PY + 8, :]
    zero_row = jnp.zeros((1, LANES), jnp.float32)
    rhs, gain, values = {}, {}, {}
    for v in range(1, 9):
        rhs[v] = packs[v][0:4] + packs[v - 1][4:8]
        gain[v] = damping / (4.0 * cy * packs[v][8:12] + base)
        values[v] = gain[v] * rhs[v]
    for sweep in range(1, CSWEEPS):
        new = {}
        for v in range(1 + sweep, 9 - sweep):
            c = values[v]
            sides = values[v - 1] + values[v + 1] + up_one(c) + down_one(c)
            walls = jnp.concatenate([zero_row, c[0:3]], axis=0) + jnp.concatenate([c[1:4], zero_row], axis=0)
            new[v] = (1.0 - damping) * c + gain[v] * (rhs[v] + cy * sides + 2.0 * walls)
        values = new
    picked = [jnp.where(second, values[v + 1], values[v]) for v in (3, 4, 5)]
    return jnp.concatenate(picked + [jnp.zeros((4, LANES), jnp.float32)], axis=0)


def tail(t, u_ref, au_ref, sm_ref, col_ref, prol_ref, ag1_ref, recv_ref, ag2_ref, z_ref, w_ref, second):
    order = [(2, 0, 32), (2, 0, 48), (2, 0, 0), (2, 0, 16), (1, 0, ROWS), (1, 1, ROWS), (2, 1, 0), (2, 1, 16), (2, 1, 32), (2, 1, 48)]
    packs = []
    for which, core, row in order:
        ref = ag1_ref if which == 1 else ag2_ref
        packs.append(ref[core, row : row + 12, :])
    c = coarse_solve(packs, col_ref, second)
    both = split_dot(prol_ref, c)
    my_rows = col_ref[0:PY, :]
    zero_planes, seven_planes = [], []
    for j in range(7):
        sib0, sib1 = ag1_ref[0, PY * j : PY * j + PY, :], ag1_ref[1, PY * j : PY * j + PY, :]
        outer = recv_ref[PY * j : PY * j + PY, :]
        zero_planes.append(my_rows * jnp.where(second, outer, sib1))
        seven_planes.append(jnp.where(second, sib0, outer))
    for i in range(7):
        f = both[plane_rows(i)]
        g = both[ROWS + PY * i : ROWS + PY * i + PY]
        f_up, g_up = up_one(f), up_one(g)
        bend = (float(t.mass[i]) * my_rows) * (f - 0.5 * (f_up + down_one(f)))
        for j in range(7):
            low, high, mass = float(t.low[j]), float(t.high[j]), float(t.mass[j])
            fine = low * f + high * f_up if j else f
            w = au_ref[plane_rows(i), tile(j)] + sm_ref[plane_rows(i), tile(j)] * fine
            w = w + ((mass * low) * g + (mass * high) * g_up if j else mass * g + bend)
            w = w + (mass * float(t.K[i, 7])) * zero_planes[j]
            if i == 0:
                w = w + seven_planes[j]
            w_ref[plane_rows(i), tile(j)] = w
            z_ref[plane_rows(i), tile(j)] = u_ref[plane_rows(i), tile(j)] + fine


def second_kernel(t, u_ref, au_ref, dinv_ref, sm_ref, col_ref, prol_ref, ag1_ref, recv_ref, ag2_ref,
                  z_ref, w_ref, u2_ref, msib_ref, xout_ref):
    core = lax.axis_index("core")
    tail(t, u_ref, au_ref, sm_ref, col_ref, prol_ref, ag1_ref, recv_ref, ag2_ref, z_ref, w_ref, core == 1)
    screen4 = jnp.where(core == 1, ag1_ref[1, ROWS + 8 : ROWS + 12, :], ag1_ref[0, ROWS + 8 : ROWS + 12, :])
    head(t, w_ref, dinv_ref, screen4, core == 0, row_tables(col_ref), u2_ref, msib_ref, xout_ref)


def third_kernel(t, w_ref, u_ref, au_ref, sm_ref, col_ref, prol_ref, ag1_ref, recv_ref, ag2_ref, sums_in_ref,
                 v_ref, y_ref, sums_ref):
    core = lax.axis_index("core")
    tail(t, u_ref, au_ref, sm_ref, col_ref, prol_ref, ag1_ref, recv_ref, ag2_ref, v_ref, y_ref, core == 1)
    groups = [sums_in_ref[0:8, :], sums_in_ref[8:16, :], partial(w_ref, v_ref), partial(v_ref, y_ref)]
    lane = lax.broadcasted_iota(jnp.int32, (1, LANES), 1) // 32
    row = jnp.zeros((1, LANES), jnp.float32)
    for k in range(4):
        total = jnp.sum(groups[k], axis=0, keepdims=True)
        total = total + pltpu.roll(total, 64, 1)
        total = total + pltpu.roll(total, 32, 1)
        row = jnp.where(lane == k, total, row)
    for g in range(sums_ref.shape[0]):
        sums_ref[g] = row


def spread_kernel(got_ref, out_ref):
    total = got_ref[0]
    for g in range(1, got_ref.shape[0]):
        total = total + got_ref[g]
    for g in range(out_ref.shape[0]):
        out_ref[g] = total


def last_kernel(rp_ref, z_ref, w_ref, v_ref, y_ref, got_ref, x_hbm, res_hbm, x_ref, res_ref, sems):
    total = got_ref[0]
    for g in range(1, got_ref.shape[0]):
        total = total + got_ref[g]
    lane = lax.broadcasted_iota(jnp.int32, (1, LANES), 1) // 32
    rho, pi, sigma, tau = [jnp.sum(jnp.where(lane == k, total, 0.0), axis=1, keepdims=True) for k in range(4)]
    step0 = rho / pi
    rho1 = step0 * step0 * sigma - rho
    ratio = 1.0 + rho1 / rho
    step1 = rho1 / (ratio * ratio * pi - 2.0 * ratio * step0 * sigma + step0 * step0 * tau)
    a = step0 + step1 * ratio
    b = step1 * step0
    copies = []
    for i in range(7):
        rows = slice(PY * i, PY * i + NY)
        x_ref[i] = a * z_ref[rows, :] - b * v_ref[rows, :]
        copies.append(pltpu.make_async_copy(x_ref.at[i], x_hbm.at[i], sems.at[0, i]))
        copies[-1].start()
        res_ref[i] = rp_ref[rows, :] - a * w_ref[rows, :] + b * y_ref[rows, :]
        copies.append(pltpu.make_async_copy(res_ref.at[i], res_hbm.at[i], sems.at[1, i]))
        copies[-1].start()
    for copy in copies:
        copy.wait()


def f32(*shape):
    return jax.ShapeDtypeStruct(shape, jnp.float32)


def call(kernel, outs, args, scratch=(), name=None, ins=pltpu.VMEM, out=pltpu.VMEM, flops=0, vmem=VMEM_BYTES):
    cost = pl.CostEstimate(flops=flops, bytes_accessed=flops // 64, transcendentals=0) if flops else None
    return pl.pallas_call(
        kernel,
        out_shape=outs,
        in_specs=[pl.BlockSpec(memory_space=ins)] * len(args),
        out_specs=[pl.BlockSpec(memory_space=out)] * len(outs) if isinstance(outs, (list, tuple)) else pl.BlockSpec(memory_space=out),
        scratch_shapes=list(scratch),
        compiler_params=pltpu.CompilerParams(vmem_limit_bytes=vmem),
        cost_estimate=cost,
        name=name,
    )(*args)


def chip_permute(block, distance):
    count = 1
    for axis in AXES:
        count *= lax.axis_size(axis)
    chips = count // 2
    route = []
    for device in range(count):
        chip, core = divmod(device, 2)
        route.append((device, 2 * ((chip + distance) % chips) if core else 2 * ((chip - distance) % chips) + 1))
    return lax.ppermute(block, AXES, route)


def halo(msib, xout):
    ag1 = lax.all_gather(msib, "core")
    packs = ag1[:, ROWS:, :].reshape(32, LANES)
    far = chip_permute(packs, 2)
    near = chip_permute(jnp.concatenate([xout, packs], axis=0), 1)
    ag2 = lax.all_gather(jnp.concatenate([near[ROWS:], far], axis=0), "core")
    return ag1, near, ag2


def per_device(right_side, screening):
    t = Tables()
    col = jnp.asarray(t.col)
    prol, wxy = (jnp.asarray(split(m)) for m in (t.prol, t.wxy))
    big = f32(ROWS, 7 * LANES)
    msg = [f32(ROWS + 16, LANES), f32(ROWS, LANES)]
    planes = pltpu.VMEM(right_side.shape, jnp.float32)
    padded = pltpu.VMEM(big.shape, jnp.float32)
    msib, xout = call(
        functools.partial(first_kernel, t), msg, (right_side, screening),
        [planes, planes] + [padded] * 4 + [pltpu.SemaphoreType.DMA((2,))], name="first", ins=pltpu.HBM, vmem=WIDE_VMEM_BYTES,
    )
    ag1, near, ag2 = halo(msib, xout)
    rp, u, dinv, sm, au = call(
        functools.partial(side_kernel, t), [big] * 5, (right_side, screening, col, wxy), name="side", flops=SIDE_FLOPS
    )
    z, w, u2, msib, xout = call(
        functools.partial(second_kernel, t), [big] * 3 + msg, (u, au, dinv, sm, col, prol, ag1, near, ag2), name="second"
    )
    ag1, near, ag2 = halo(msib, xout)
    au2, sums = call(
        functools.partial(side_sums_kernel, t), [big, f32(16, LANES)], (u2, sm, col, wxy, rp, z, w), name="side_sums", flops=SIDE_FLOPS
    )
    groups = lax.axis_size(("x", "y"))
    rest_count = lax.axis_size(("z", "core"))
    v, y, sums = call(
        functools.partial(third_kernel, t), [big, big, f32(groups, 1, LANES)],
        (w, u2, au2, sm, col, prol, ag1, near, ag2, sums), name="third",
    )
    got = lax.all_to_all(sums, ("x", "y"), 0, 0, tiled=True)
    sums = call(spread_kernel, f32(rest_count, 1, LANES), (got,), name="spread")
    got = lax.all_to_all(sums, ("z", "core"), 0, 0, tiled=True)
    return call(
        last_kernel, [f32(*right_side.shape)] * 2, (rp, z, w, v, y, got),
        [planes, planes, pltpu.SemaphoreType.DMA((2, 7))], name="last", out=pltpu.HBM,
    )


def solution(mesh):
    devices = np.asarray(mesh.devices)
    shape = GRID.get(devices.size) or (1, 1, devices.size // 2, 2)
    fine_mesh = Mesh(devices.reshape(shape), AXES)
    spec = P(AXES, None, None)
    return jax.shard_map(per_device, mesh=fine_mesh, in_specs=(spec, spec), out_specs=(spec, spec), check_vma=False)
```

time: 90.1 us -> 85.2 us (0.946)
  local copies, waits for them, and re-layouts: 4.45 us -> 0.03 us
  waiting for transfers between devices: 8.05 us -> 6.19 us
  Pallas kernels: 4.99 us -> 6.55 us
    unnamed x18 -> x10, local copies, waits for them, and re-layouts: 4.44 us -> 0.03 us
    ppermute x4, waiting for transfers between devices: 8.05 us -> 6.19 us  [chip_permute(): return lax.ppermute(block, AXES, route)]
    pallas_call x5 -> x7, Pallas kernels: 4.99 us -> 6.55 us  [call(): pl.pallas_call(kernel, out_shape=outs, in_specs=[pl.BlockSpec(memory_spac...]
  transfers between devices with their start and end apart: 4 -> 4, of which waited for: 4 -> 4; matrix products, arithmetic and copies ran while one was open for 0% -> 0% of each run, Pallas kernels for 0% -> 2%
where the time goes in v2:
time: 85.2 us; the launch traced here: 84.9 us
  blocking collectives  63.5 us (75%)
  starting transfers between devices  7.81 us (9%)
  Pallas kernels  6.55 us (8%)
  waiting for transfers between devices  6.19 us (7%)
    all_gather x2, blocking collectives, halo(): ag2 = lax.all_gather(jnp.concatenate([near[ROWS:], far], axis=0), 'core')  23.1 us
    all_to_all x1, blocking collectives, per_device(): got = lax.all_to_all(sums, ('z', 'core'), 0, 0, tiled=True)  20.9 us
    all_gather x2, blocking collectives, halo(): ag1 = lax.all_gather(msib, 'core')  10.5 us
    all_to_all x1, blocking collectives, per_device(): got = lax.all_to_all(sums, ('x', 'y'), 0, 0, tiled=True)  8.95 us
    ppermute x4, starting transfers between devices, chip_permute(): return lax.ppermute(block, AXES, route)  7.81 us
    pallas_call x7, Pallas kernels, call(): pl.pallas_call(kernel, out_shape=outs, in_specs=[pl.BlockSpec(memory_spac...  6.55 us
    ppermute x4, waiting for transfers between devices, chip_permute(): return lax.ppermute(block, AXES, route)  6.19 us
  transfers between devices with their start and end apart: 4, of which 4 were waited for; matrix products, arithmetic and copies ran while one was open for 0% of the time, Pallas kernels for 2%

profile of v2, /device:TPU:1, one launch (start us, length us, event | category | flops | bytes accessed | tf_op | source)
XLA Modules:
  0.0 84.9 jit_solution(13897117027171961800)
XLA Ops:
  0.6 1.6 %first.1 = (f32[184,128]{1,0:T(8,128)S(1)}, f32[168,128]{1,0:T(8,128)S(1)}) custom-call(f32[7,22,896]{2,1,0:T(8,128)} %r_hbm.1, f32[7,22,896]{2,1,0:T(8,128)} %s_hbm.1), custom_call_target="tpu_custom_call" | custom-call | tf_op jit(solution)/shard_map/first/pallas_call | solution.py:405
  2.2 0.0 copy-start.4
  2.2 8.6 %all-gather = f32[368,128]{1,0:T(8,128)S(1)} all-gather(f32[184,128]{1,0:T(8,128)S(1)} %get-tuple-element.24), channel_id=2, replica_groups=mesh['x'=4,'y'=4,'z'=16,'core'=2] {'core'}, dimensions={0}, use_global_device_ids=true | all-gather | bytes 282624 | tf_op jit(solution)/shard_map/all_gather | solution.py:430
  10.9 2.1 %collective-permute-start = (f32[200,128]{1,0:T(8,128)S(1)}, f32[200,128]{1,0:T(8,128)S(1)}, u32[]{:S(2)}, u32[]{:S(2)}) collective-permute-start(f32[200,128]{1,0:T(8,128)S(1)} %pad_maximum_fusion), channel_id=1, source_target_pairs={{0,511},{1,2},{2,1},{3,4},{4,3},{5,6},{6,5},{7,8},{8,7},{9,10},{10... | collective-permute-start | bytes 307208 | tf_op jit(solution)/shard_map/ppermute | solution.py:426
  12.9 1.9 %collective-permute-start.1 = (f32[32,128]{1,0:T(8,128)S(1)}, f32[32,128]{1,0:T(8,128)S(1)}, u32[]{:S(2)}, u32[]{:S(2)}) collective-permute-start(f32[32,128]{1,0:T(8,128)S(1)} %bitcast.13), channel_id=1, source_target_pairs={{0,509},{1,4},{2,511},{3,6},{4,1},{5,8},{6,3},{7,10},{8,5},{9,12},... | collective-permute-start | bytes 49160 | tf_op jit(solution)/shard_map/ppermute | solution.py:426
  14.8 0.0 copy-done.3
  14.9 0.0 copy-done.2
  14.9 0.9 %side.1 = (f32[168,896]{1,0:T(8,128)S(1)}, f32[168,896]{1,0:T(8,128)S(1)}, f32[168,896]{1,0:T(8,128)S(1)}, f32[168,896]{1,0:T(8,128)S(1)}, f32[168,896]{1,0:T(8,128)S(1)}) custom-call(f32[7,22,896]{2,1,0:T(8,128)S(1)} %copy-done.2, f32[7,22,896]{2,1,0:T(8,128)S(1)} %copy-done.3, f32[176,128]{1,0:T(8,128)S(1)} %copy-done, bf16[2,168,168]{2,1,0:T(8,128)(2,1)S(1)} %copy-done.4), custom_call_target="tpu_custom_call" | custom-call | flops 500000000 | bytes 7812500 | tf_op jit(solution)/shard_map/side/pallas_call | solution.py:405
  15.8 0.0 copy-start.1
  15.8 1.2 %collective-permute-done.recv_ref = f32[200,128]{1,0:T(8,128)S(1)} collective-permute-done((f32[200,128]{1,0:T(8,128)S(1)}, f32[200,128]{1,0:T(8,128)S(1)}, u32[]{:S(2)}, u32[]{:S(2)}) %collective-permute-start) | collective-permute-done | bytes 102432 | tf_op jit(solution)/shard_map/ppermute | solution.py:426
  17.0 1.9 %collective-permute-done.1 = f32[32,128]{1,0:T(8,128)S(1)} collective-permute-done((f32[32,128]{1,0:T(8,128)S(1)}, f32[32,128]{1,0:T(8,128)S(1)}, u32[]{:S(2)}, u32[]{:S(2)}) %collective-permute-start.1) | collective-permute-done | bytes 16416 | tf_op jit(solution)/shard_map/ppermute | solution.py:426
  18.9 15.8 %all-gather.1 = f32[128,128]{1,0:T(8,128)S(1)} all-gather(f32[64,128]{1,0:T(8,128)S(1)} %pad_maximum_fusion.2), channel_id=3, replica_groups=mesh['x'=4,'y'=4,'z'=16,'core'=2] {'core'}, dimensions={0}, use_global_device_ids=true | all-gather | bytes 98304 | tf_op jit(solution)/shard_map/all_gather | solution.py:434
  34.7 0.9 %second.1 = (f32[168,896]{1,0:T(8,128)S(1)}, f32[168,896]{1,0:T(8,128)S(1)}, f32[168,896]{1,0:T(8,128)S(1)}, f32[184,128]{1,0:T(8,128)S(1)}, f32[168,128]{1,0:T(8,128)S(1)}) custom-call(f32[168,896]{1,0:T(8,128)S(1)} %get-tuple-element.20.u_ref, f32[168,896]{1,0:T(8,128)S(1)} %get-tuple-element.21.au_ref, f32[168,896]{1,0:T(8,128)S(1)} %get-tuple-element.22.dinv_ref, ...), custom_call_target="tpu_custom_call" | custom-call | tf_op jit(solution)/shard_map/second/pallas_call | solution.py:405
  35.6 1.9 %all-gather.2 = f32[368,128]{1,0:T(8,128)S(1)} all-gather(f32[184,128]{1,0:T(8,128)S(1)} %get-tuple-element.30), channel_id=4, replica_groups=mesh['x'=4,'y'=4,'z'=16,'core'=2] {'core'}, dimensions={0}, use_global_device_ids=true | all-gather | bytes 282624 | tf_op jit(solution)/shard_map/all_gather | solution.py:430
  37.5 1.9 %collective-permute-start.2 = (f32[200,128]{1,0:T(8,128)S(1)}, f32[200,128]{1,0:T(8,128)S(1)}, u32[]{:S(2)}, u32[]{:S(2)}) collective-permute-start(f32[200,128]{1,0:T(8,128)S(1)} %pad_maximum_fusion.1), channel_id=1, source_target_pairs={{0,511},{1,2},{2,1},{3,4},{4,3},{5,6},{6,5},{7,8},{8,7},{9,10},{10... | collective-permute-start | bytes 307208 | tf_op jit(solution)/shard_map/ppermute | solution.py:426
  39.5 1.9 %collective-permute-start.3 = (f32[32,128]{1,0:T(8,128)S(1)}, f32[32,128]{1,0:T(8,128)S(1)}, u32[]{:S(2)}, u32[]{:S(2)}) collective-permute-start(f32[32,128]{1,0:T(8,128)S(1)} %bitcast.15), channel_id=1, source_target_pairs={{0,509},{1,4},{2,511},{3,6},{4,1},{5,8},{6,3},{7,10},{8,5},{9,12},... | collective-permute-start | bytes 49160 | tf_op jit(solution)/shard_map/ppermute | solution.py:426
  41.4 0.9 %side_sums.1 = (f32[168,896]{1,0:T(8,128)S(1)}, f32[16,128]{1,0:T(8,128)S(1)}) custom-call(f32[168,896]{1,0:T(8,128)S(1)} %get-tuple-element.28.u_ref, f32[168,896]{1,0:T(8,128)S(1)} %get-tuple-element.23.sm_ref, f32[176,128]{1,0:T(8,128)S(1)} %copy-done, bf16[2,168,168]{2,1,0:T(8,128)(2,1)S(1)} %copy-done.4, f32[168,896]{1,0:T(8,128)S(1)} %get-tuple-element.19.rp_ref, ...), custom_call_target="tpu_custom_call" | custom-call | flops 500000000 | bytes 7812500 | tf_op jit(solution)/shard_map/side_sums/pallas_call | solution.py:405
  42.3 1.2 %collective-permute-done.2.recv_ref = f32[200,128]{1,0:T(8,128)S(1)} collective-permute-done((f32[200,128]{1,0:T(8,128)S(1)}, f32[200,128]{1,0:T(8,128)S(1)}, u32[]{:S(2)}, u32[]{:S(2)}) %collective-permute-start.2) | collective-permute-done | bytes 102432 | tf_op jit(solution)/shard_map/ppermute | solution.py:426
  43.5 1.9 %collective-permute-done.3 = f32[32,128]{1,0:T(8,128)S(1)} collective-permute-done((f32[32,128]{1,0:T(8,128)S(1)}, f32[32,128]{1,0:T(8,128)S(1)}, u32[]{:S(2)}, u32[]{:S(2)}) %collective-permute-start.3) | collective-permute-done | bytes 16416 | tf_op jit(solution)/shard_map/ppermute | solution.py:426
  45.4 7.3 %all-gather.3 = f32[128,128]{1,0:T(8,128)S(1)} all-gather(f32[64,128]{1,0:T(8,128)S(1)} %pad_maximum_fusion.3), channel_id=5, replica_groups=mesh['x'=4,'y'=4,'z'=16,'core'=2] {'core'}, dimensions={0}, use_global_device_ids=true | all-gather | bytes 98304 | tf_op jit(solution)/shard_map/all_gather | solution.py:434
  52.7 1.0 %third.1 = (f32[168,896]{1,0:T(8,128)S(1)}, f32[168,896]{1,0:T(8,128)S(1)}, f32[16,1,128]{2,1,0:T(1,128)S(1)}) custom-call(f32[168,896]{1,0:T(8,128)S(1)} %get-tuple-element.27.w_ref, f32[168,896]{1,0:T(8,128)S(1)} %get-tuple-element.28.u_ref, f32[168,896]{1,0:T(8,128)S(1)} %get-tuple-element.29.au_ref, f32[168,896]{1,0:T(8,128)S(1)} %get-tuple-element.23.sm_ref, ...), custom_call_target="tpu_custom_call" | custom-call | tf_op jit(solution)/shard_map/third/pallas_call | solution.py:405
  53.7 9.0 %all_to_all.10.got_ref = f32[16,1,128]{2,1,0:T(1,128)S(1)} all-to-all(f32[16,1,128]{2,1,0:T(1,128)S(1)} %get-tuple-element.35), channel_id=1, replica_groups=mesh['x'=4,'y'=4,'z'=16,'core'=2] {'x','y'}, dimensions={0} | all-to-all | bytes 16384 | tf_op jit(solution)/shard_map/all_to_all | solution.py:467
  62.7 20.9 %all_to_all.11.got_ref = f32[32,1,128]{2,1,0:T(1,128)S(1)} all-to-all(f32[32,1,128]{2,1,0:T(1,128)S(1)} %spread.1), channel_id=1, replica_groups=mesh['x'=4,'y'=4,'z'=16,'core'=2] {'z','core'}, dimensions={0} | all-to-all | bytes 32768 | tf_op jit(solution)/shard_map/all_to_all | solution.py:469
  83.6 1.3 %last.1 = (f32[7,22,896]{2,1,0:T(8,128)}, f32[7,22,896]{2,1,0:T(8,128)}) custom-call(f32[168,896]{1,0:T(8,128)S(1)} %get-tuple-element.19.rp_ref, f32[168,896]{1,0:T(8,128)S(1)} %get-tuple-element.26.z_ref, f32[168,896]{1,0:T(8,128)S(1)} %get-tuple-element.27.w_ref, f32[168,896]{1,0:T(8,128)S(1)} %get-tuple-element.33.v_ref, ...), custom_call_target="tpu_custom_call" | custom-call | tf_op jit(solution)/shard_map/last/pallas_call | solution.py:405
  (15 shorter events, 0.1 us)
Async XLA Ops:
  0.6 14.2 %copy-start.3 = (f32[7,22,896]{2,1,0:T(8,128)S(1)}, f32[7,22,896]{2,1,0:T(8,128)}, u32[]{:S(2)}) copy-start(f32[7,22,896]{2,1,0:T(8,128)} %s_hbm.1) | copy-start | bytes 1655812
  0.6 14.2 %copy-start.2 = (f32[7,22,896]{2,1,0:T(8,128)S(1)}, f32[7,22,896]{2,1,0:T(8,128)}, u32[]{:S(2)}) copy-start(f32[7,22,896]{2,1,0:T(8,128)} %r_hbm.1) | copy-start | bytes 1655812
  2.2 12.6 %copy-start.4 = (bf16[2,168,168]{2,1,0:T(8,128)(2,1)S(1)}, bf16[2,168,168]{2,1,0:T(8,128)(2,1)}, u32[]{:S(2)}) copy-start(bf16[2,168,168]{2,1,0:T(8,128)(2,1)} %constant.8.clone.wxy_ref) | copy-start | bytes 338692
  10.8 4.0 %copy-start = (f32[176,128]{1,0:T(8,128)S(1)}, f32[176,128]{1,0:T(8,128)}, u32[]{:S(2)}) copy-start(f32[176,128]{1,0:T(8,128)} %constant.6.clone.col_ref) | copy-start | bytes 270340
  10.9 6.1 %collective-permute-start = (f32[200,128]{1,0:T(8,128)S(1)}, f32[200,128]{1,0:T(8,128)S(1)}, u32[]{:S(2)}, u32[]{:S(2)}) collective-permute-start(f32[200,128]{1,0:T(8,128)S(1)} %pad_maximum_fusion), channel_id=1, source_target_pairs={{0,511},{1,2},{2,1},{3,4},{4,3},{5,6},{6,5},{7,8},{8,7},{9,10},{10... | collective-permute-start | bytes 307208 | tf_op jit(solution)/shard_map/ppermute | solution.py:426
  12.9 6.0 %collective-permute-start.1 = (f32[32,128]{1,0:T(8,128)S(1)}, f32[32,128]{1,0:T(8,128)S(1)}, u32[]{:S(2)}, u32[]{:S(2)}) collective-permute-start(f32[32,128]{1,0:T(8,128)S(1)} %bitcast.13), channel_id=1, source_target_pairs={{0,509},{1,4},{2,511},{3,6},{4,1},{5,8},{6,3},{7,10},{8,5},{9,12},... | collective-permute-start | bytes 49160 | tf_op jit(solution)/shard_map/ppermute | solution.py:426
  15.8 18.9 %copy-start.1 = (bf16[2,336,16]{2,1,0:T(8,128)(2,1)S(1)}, bf16[2,336,16]{2,1,0:T(8,128)(2,1)}, u32[]{:S(2)}) copy-start(bf16[2,336,16]{2,1,0:T(8,128)(2,1)} %constant.7.clone.prol_ref) | copy-start | bytes 64516
  37.5 6.0 %collective-permute-start.2 = (f32[200,128]{1,0:T(8,128)S(1)}, f32[200,128]{1,0:T(8,128)S(1)}, u32[]{:S(2)}, u32[]{:S(2)}) collective-permute-start(f32[200,128]{1,0:T(8,128)S(1)} %pad_maximum_fusion.1), channel_id=1, source_target_pairs={{0,511},{1,2},{2,1},{3,4},{4,3},{5,6},{6,5},{7,8},{8,7},{9,10},{10... | collective-permute-start | bytes 307208 | tf_op jit(solution)/shard_map/ppermute | solution.py:426
  39.5 6.0 %collective-permute-start.3 = (f32[32,128]{1,0:T(8,128)S(1)}, f32[32,128]{1,0:T(8,128)S(1)}, u32[]{:S(2)}, u32[]{:S(2)}) collective-permute-start(f32[32,128]{1,0:T(8,128)S(1)} %bitcast.15), channel_id=1, source_target_pairs={{0,509},{1,4},{2,511},{3,6},{4,1},{5,8},{6,3},{7,10},{8,5},{9,12},... | collective-permute-start | bytes 49160 | tf_op jit(solution)/shard_map/ppermute | solution.py:426
